TPU v7x, 128 devices: a whole 4x4x4 slice. The times are simulated.
128 devices in a mesh: tile: 16 (over x, y), lat: 8 (over z, core).
Axes of the slice: x: 4, y: 4, z: 4, core: 2. Of those that a mesh axis runs over, the one named last changes fastest.
Arguments:
- source: bfloat16 [896, 8, 4096], P(('tile', 'lat')), may hold values from -6 to 6
- row_map: bfloat16 [40, 16, 4, 32, 64], P('lat', 'tile'), may hold values from -0.375 to 0.375
- col_map: bfloat16 [40, 4, 64, 2560], P('lat', None, None, 'tile'), may hold values from -0.75 to 0.75
- pattern: int32 [40, 16, 4], P('lat', 'tile'), may hold values from 0 to 11, as said below
- codes: int32 [40, 16, 4], P('lat', 'tile'), may hold values from 0 to 3
- need_list: int32 [16, 8, 12], P('tile'), may hold values from 0 to 895, as said below
- owner: int32 [896], replicated, may hold values from 0 to 895, as said below
Outputs:
- spectrum: float32 [640, 16, 1281], P(('tile', 'lat'))
Inputs may be any that keep to these rules, and one draw needn't show every extreme that they name: need_list[t, l] names 12 distinct blocks, all held by devices of tile column t; each device that holds any of them holds exactly 3 of them. `owner`: a permutation of the slots. `pattern`: on each device every one of the 12 indices is used by some term.
All inputs are finite; a program needn't handle non-finite values.
Results may differ from a plain program's by a relative error of at most 0.0029.
Values may be sent and summed in bfloat16 or wider, within the bound.
No kernel may reach another device: no remote copies, remote signals or barrier semaphores. Data moves between devices by JAX's collectives and lax.ppermute only.
A program may use at most 64 MiB of HBM per device.

v0:
```python
import math

import jax
import jax.numpy as jnp
from jax import lax
from jax.sharding import PartitionSpec as P

NLON = 2560
NLAT = 1280
M = 1280
NEED = 12
MOST = 3
LEV = 8


highest = lax.Precision.HIGHEST


def sectoral_logs():
    steps = jnp.arange(1, M, dtype=jnp.int32).astype(jnp.float32)
    terms = 0.5 * jnp.log1p(0.5 / steps)
    return jnp.concatenate([jnp.zeros((1,), jnp.float32), jnp.cumsum(terms)]) + 0.5 * math.log(0.5)


def legendre_sums(fields, pair_ids, colat, weights):
    count = pair_ids.shape[0]
    lats = colat.shape[0]
    norm_logs = sectoral_logs()
    orders = jnp.arange(M, dtype=jnp.int32)
    high_order = M - 1 - pair_ids
    low_length = M - pair_ids
    cosine = jnp.cos(colat)
    log_sine = jnp.log(jnp.sin(colat))

    def sectoral(order):
        picked = jnp.sum(
            jnp.where(order[:, None] == orders[None, :], norm_logs[None, :], 0.0), axis=1
        )
        exponent = picked[:, None] + order.astype(jnp.float32)[:, None] * log_sine[None, :]
        ramp = jnp.clip((exponent + 75.0) / 10.0, 0.0, 1.0)
        return jnp.exp(jnp.maximum(exponent, -75.0)) * ramp

    start_low = sectoral(pair_ids)
    start_high = sectoral(high_order)
    scaled = fields * weights[None, None, :, None]

    def advance(state, slot):
        previous, before = state
        is_low = slot < low_length
        order = jnp.where(is_low, pair_ids, high_order)
        degree = jnp.where(is_low, pair_ids + slot, high_order + slot - low_length)
        fresh = degree == order
        order_f = order.astype(jnp.float32)
        degree_f = degree.astype(jnp.float32)
        lower_f = degree_f - 1.0
        grows = degree > order
        ratio = jnp.where(
            grows,
            (4.0 * degree_f * degree_f - 1.0)
            / jnp.where(grows, degree_f * degree_f - order_f * order_f, 1.0),
            0.0,
        )
        back = degree - 1 > order
        inverse = jnp.where(
            back,
            (lower_f * lower_f - order_f * order_f)
            / jnp.where(back, 4.0 * lower_f * lower_f - 1.0, 1.0),
            0.0,
        )
        grown = jnp.sqrt(ratio)[:, None] * (
            cosine[None, :] * previous - jnp.sqrt(inverse)[:, None] * before
        )
        start = jnp.where(is_low[:, None], start_low, start_high)
        value = jnp.where(fresh[:, None], start, grown)
        return ((value, jnp.where(fresh[:, None], 0.0, previous)), value)

    def one_block(state, base):
        slots = base + jnp.arange(128, dtype=jnp.int32)
        state, table = lax.scan(advance, state, slots, unroll=8)
        low_mask = (slots[:, None] < low_length[None, :]).astype(jnp.float32)
        both = jnp.stack(
            [table * low_mask[:, :, None], table * (1.0 - low_mask)[:, :, None]], axis=2
        )
        sums = jnp.einsum("sqhl,qhlc->qcs", both, scaled, precision=highest)
        return (state, sums)

    zeros = jnp.zeros((count, lats), jnp.float32)
    total = -(-(M + 1) // 128)
    bases = jnp.arange(total, dtype=jnp.int32) * 128
    _, sums = lax.scan(one_block, (zeros, zeros), bases)
    sums = jnp.transpose(sums, (1, 2, 0, 3)).reshape(count, fields.shape[3], total * 128)
    return sums[:, :, : M + 1]


def row_products(picked, code, rmap, cmap):
    side = rmap.shape[2]
    blocks = picked.reshape(picked.shape[0], picked.shape[1], side, side)
    turned = jnp.swapaxes(blocks, 2, 3)
    chosen = jnp.where((code % 2 == 1)[:, None, None, None], turned, blocks)
    row_flip = (code == 1) | (code == 2)
    col_flip = (code == 2) | (code == 3)
    rmap = jnp.where(row_flip[:, None, None], rmap[:, :, ::-1], rmap)
    cmap = jnp.where(col_flip[:, None, None], cmap[:, ::-1, :], cmap)
    inner = jnp.einsum("klrc,kcx->klrx", chosen, cmap, preferred_element_type=jnp.float32).astype(
        jnp.bfloat16
    )
    return jnp.einsum("kar,klrx->lax", rmap, inner, preferred_element_type=jnp.float32)


def dft_table(base):
    columns = base + jnp.arange(256, dtype=jnp.int32)
    pair_index = columns // 4
    upper = columns // 2 % 2
    parity = columns % 2
    order = jnp.where(upper == 0, pair_index, M - 1 - pair_index)
    points = jnp.arange(NLON, dtype=jnp.int32)
    phase = points[:, None] * order[None, :] % NLON
    angle = phase.astype(jnp.float32) * (2.0 * math.pi / NLON)
    return jnp.where(parity[None, :] == 0, jnp.cos(angle), -jnp.sin(angle)) / math.sqrt(NLON)


def body(source, row_map, col_map, pattern, codes, need_list, owner):
    lat_count = lax.axis_size("lat")
    tile_count = lax.axis_size("tile")
    lat_me = lax.axis_index("lat")
    tile_me = lax.axis_index("tile")
    slots_dev = source.shape[0]
    block_ids = jnp.arange(owner.shape[0], dtype=jnp.int32)
    needs_column = need_list[0]
    holder = jnp.sum(
        jnp.where(needs_column[:, :, None] == block_ids[None, None, :], owner[None, None, :], 0),
        axis=2,
    )
    holder_lat = holder // slots_dev % lat_count
    holder_slot = holder % slots_dev
    my_lat = lax.dynamic_index_in_dim(holder_lat, lat_me, 0, keepdims=False)
    held_here = holder_lat == lat_me
    rank = jnp.cumsum(held_here.astype(jnp.int32), axis=1) - 1
    places = jnp.arange(MOST, dtype=jnp.int32)
    hit = held_here[:, None, :] & (rank[:, None, :] == places[None, :, None])
    picks = jnp.sum(jnp.where(hit, holder_slot[:, None, :], 0), axis=2)
    outgoing = jnp.take(source, picks.reshape(-1), axis=0).reshape(
        (lat_count, MOST) + source.shape[1:]
    )
    incoming = lax.all_to_all(outgoing, "lat", split_axis=0, concat_axis=0, tiled=True)
    earlier = jnp.arange(NEED)[:, None] > jnp.arange(NEED)[None, :]
    same = (my_lat[:, None] == my_lat[None, :]) & earlier
    my_rank = jnp.sum(same.astype(jnp.int32), axis=1)
    flat = incoming.reshape((lat_count * MOST,) + source.shape[1:])
    gathered = jnp.take(flat, my_lat * MOST + my_rank, axis=0)

    def one_row(inputs):
        index, code, rmap, cmap = inputs
        return row_products(jnp.take(gathered, index, axis=0), code, rmap, cmap)

    rows = lax.map(one_row, (pattern[:, 0], codes[:, 0], row_map[:, 0], col_map))
    field = jnp.transpose(rows, (1, 0, 2, 3)).reshape(
        rows.shape[1], rows.shape[0] * rows.shape[2], rows.shape[3]
    )
    lat_rows = lax.all_to_all(field, "tile", split_axis=1, concat_axis=2, tiled=True)
    levels = lat_rows.shape[0]
    count = lat_rows.shape[1]
    flat_rows = lat_rows.reshape(levels * count, NLON)

    def one_columns(base):
        return jnp.dot(flat_rows, dft_table(base), precision=highest)

    blocks = lax.map(one_columns, jnp.arange(2 * M // 256, dtype=jnp.int32) * 256)
    spectral = jnp.transpose(blocks, (1, 0, 2)).reshape(levels, count, 2 * M)
    arranged = lax.all_to_all(spectral, ("tile", "lat"), split_axis=2, concat_axis=1, tiled=True)
    pairs_dev = M // 2 // (lat_count * tile_count)
    spread_rows = NLAT // (lat_count * tile_count)
    positions = jnp.arange(NLAT, dtype=jnp.int32)
    group = positions // spread_rows
    latitude = (
        group % lat_count * (NLAT // lat_count)
        + group // lat_count * spread_rows
        + positions % spread_rows
    )
    colat = math.pi * (latitude.astype(jnp.float32) + 0.75) / (NLAT + 0.5)
    weights = math.pi * jnp.sin(colat) * math.sqrt(NLAT) / (NLAT + 0.5)
    fields = arranged.reshape(LEV, NLAT, pairs_dev, 2, 2)
    fields = jnp.transpose(fields, (2, 3, 1, 4, 0)).reshape(pairs_dev, 2, NLAT, 2 * LEV)
    pair_ids = (tile_me * lat_count + lat_me) * pairs_dev + jnp.arange(pairs_dev, dtype=jnp.int32)
    return legendre_sums(fields, pair_ids, colat, weights)


def solution(mesh):
    placed = (
        P(("tile", "lat"), None, None),
        P("lat", "tile", None, None, None),
        P("lat", None, None, "tile"),
        P("lat", "tile", None),
        P("lat", "tile", None),
        P("tile", None, None),
        P(),
    )
    return jax.shard_map(
        body, mesh=mesh, in_specs=placed, out_specs=P(("tile", "lat"), None, None), check_vma=False
    )
```

profile of v0, /device:TPU:1, one launch (start us, length us, event | category | flops | bytes accessed | tf_op | source)
XLA Modules:
  0.0 1899.6 jit_solution(12317862868269230766)
XLA Ops:
  4.7 6.8 all-to-all-start
  12.1 20.1 %all-to-all-done = bf16[8,3,8,4096]{3,2,1,0:T(8,128)(2,1)S(1)} async-done(((bf16[8,3,8,4096]{3,2,1,0:T(8,128)(2,1)}), bf16[8,3,8,4096]{3,2,1,0:T(8,128)(2,1)S(1)}, u32[]{:S(2)}, u32[]{:S(2)}) %all-to-all-start) | async-done | bytes 1572896 | tf_op jit(solution)/shard_map/all_to_all | solution.py:145
  35.0 28.7 %while.76 = (s32[]{:T(128)}, f32[5,8,32,160]{3,2,0,1:T(8,128)}, s32[5,4]{1,0:T(8,128)S(1)}, s32[5,4]{1,0:T(8,128)S(1)}, bf16[12,8,4096]{2,1,0:T(8,128)(2,1)S(1)}...) while((s32[]{:T(128)}, f32[5,8,32,160]{3,2,0,1:T(8,128)}, ...), condition=%wide.region_9.10_spmd, body=%wide.region_8.9_spmd.sunk | while | flops 63685736 | bytes 3544809 | solution.py:156
  66.9 6.8 all-to-all-start.1
  73.7 17.9 all-to-all-done.1
  93.3 156.4 %while.77 = (s32[]{:T(128)}, f32[10,80,256]{2,1,0:T(8,128)}, s32[10]{0:T(128)S(1)}, f32[80,2560]{1,0:T(8,128)S(1)}, s32[]{:T(128)}) while((s32[]{:T(128)}, f32[10,80,256]{2,1,0:T(8,128)}, s32[10]{0:T(128)S(1)}, f32[80,2560]{1,0:T(8,128)S(1)}, s32[]{:T(128)}) %tuple.253), condition=%wide.region_11.12_spmd, body=%wide.region_10.11_spmd.sunk | while | flops 637023488 | bytes 904273 | solution.py:168
  95.4 13.6 fusion.254
  111.0 13.6 fusion.254
  126.7 13.6 fusion.254
  142.3 13.6 fusion.254
  157.9 13.6 fusion.254
  173.6 13.6 fusion.254
  189.2 13.6 fusion.254
  204.9 13.6 fusion.254
  220.5 13.6 fusion.254
  236.2 13.6 fusion.254
  251.3 5.9 reshape.1090
  257.1 11.3 reshape.1094
  268.5 7.2 all-to-all-start.2
  276.7 16.3 all-to-all-done.2
  296.2 12.9 reshape.1095
  309.1 13.9 copy.84
  323.0 8.4 reshape.1056
  331.5 1567.3 %while.79 = (s32[]{:T(128)}, f32[5,1280]{1,0:T(8,128)S(1)}, f32[5,1280]{1,0:T(8,128)S(1)}, f32[11,5,16,128]{3,2,1,0:T(8,128)S(1)}, s32[11]{0:T(128)S(1)}, /*inde...) while((s32[]{:T(128)}, f32[5,1280]{1,0:T(8,128)S(1)}, ...), condition=%wide.region_15.16_spmd.clone.clone.clone, body=%wide.region_12.15_spmd.clone.clone.clone.sunk | while | flops 319516000 | bytes 19613644 | solution.py:90
  333.1 132.4 %while.80 = (s32[]{:T(128)}, f32[5,1280]{1,0:T(8,128)S(1)}, f32[5,1280]{1,0:T(8,128)S(1)}, f32[16,8,5,1280]{3,1,0,2:T(8,128)}, s32[16,8]{0,1:T(8,128)S(1)}, /*in...) while((s32[]{:T(128)}, f32[5,1280]{1,0:T(8,128)S(1)}, ...), condition=%wide.region_14.14_spmd.clone, body=%wide.region_13.13_spmd.clone.sunk | while | flops 1524421 | bytes 2295300 | solution.py:79
  333.8 4.9 broadcast_compare_fusion.12
  342.1 4.9 broadcast_compare_fusion.12
  366.9 4.9 broadcast_compare_fusion.12
  375.2 4.9 broadcast_compare_fusion.12
  383.5 4.9 broadcast_compare_fusion.12
  391.8 4.9 broadcast_compare_fusion.12
  400.0 4.9 broadcast_compare_fusion.12
  468.6 5.6 fusion.258
  475.6 132.4 %while.80 = (s32[]{:T(128)}, f32[5,1280]{1,0:T(8,128)S(1)}, f32[5,1280]{1,0:T(8,128)S(1)}, f32[16,8,5,1280]{3,1,0,2:T(8,128)}, s32[16,8]{0,1:T(8,128)S(1)}, /*in...) while((s32[]{:T(128)}, f32[5,1280]{1,0:T(8,128)S(1)}, ...), condition=%wide.region_14.14_spmd.clone, body=%wide.region_13.13_spmd.clone.sunk | while | flops 1524421 | bytes 2295300 | solution.py:79
  492.8 4.9 broadcast_compare_fusion.12
  501.1 4.9 broadcast_compare_fusion.12
  534.2 4.9 broadcast_compare_fusion.12
  542.5 4.9 broadcast_compare_fusion.12
  583.8 4.9 broadcast_compare_fusion.12
  611.1 5.6 fusion.258
  618.0 132.4 %while.80 = (s32[]{:T(128)}, f32[5,1280]{1,0:T(8,128)S(1)}, f32[5,1280]{1,0:T(8,128)S(1)}, f32[16,8,5,1280]{3,1,0,2:T(8,128)}, s32[16,8]{0,1:T(8,128)S(1)}, /*in...) while((s32[]{:T(128)}, f32[5,1280]{1,0:T(8,128)S(1)}, ...), condition=%wide.region_14.14_spmd.clone, body=%wide.region_13.13_spmd.clone.sunk | while | flops 1524421 | bytes 2295300 | solution.py:79
  627.0 4.9 broadcast_compare_fusion.12
  693.2 4.9 broadcast_compare_fusion.12
  701.5 4.9 broadcast_compare_fusion.12
  709.7 4.9 broadcast_compare_fusion.12
  718.0 4.9 broadcast_compare_fusion.12
  734.5 4.9 broadcast_compare_fusion.12
  753.6 5.6 fusion.258
  760.5 132.4 %while.80 = (s32[]{:T(128)}, f32[5,1280]{1,0:T(8,128)S(1)}, f32[5,1280]{1,0:T(8,128)S(1)}, f32[16,8,5,1280]{3,1,0,2:T(8,128)}, s32[16,8]{0,1:T(8,128)S(1)}, /*in...) while((s32[]{:T(128)}, f32[5,1280]{1,0:T(8,128)S(1)}, ...), condition=%wide.region_14.14_spmd.clone, body=%wide.region_13.13_spmd.clone.sunk | while | flops 1524421 | bytes 2295300 | solution.py:79
  896.0 5.6 fusion.258
  903.0 132.4 %while.80 = (s32[]{:T(128)}, f32[5,1280]{1,0:T(8,128)S(1)}, f32[5,1280]{1,0:T(8,128)S(1)}, f32[16,8,5,1280]{3,1,0,2:T(8,128)}, s32[16,8]{0,1:T(8,128)S(1)}, /*in...) while((s32[]{:T(128)}, f32[5,1280]{1,0:T(8,128)S(1)}, ...), condition=%wide.region_14.14_spmd.clone, body=%wide.region_13.13_spmd.clone.sunk | while | flops 1524421 | bytes 2295300 | solution.py:79
  1038.5 5.6 fusion.258
  1045.4 132.4 %while.80 = (s32[]{:T(128)}, f32[5,1280]{1,0:T(8,128)S(1)}, f32[5,1280]{1,0:T(8,128)S(1)}, f32[16,8,5,1280]{3,1,0,2:T(8,128)}, s32[16,8]{0,1:T(8,128)S(1)}, /*in...) while((s32[]{:T(128)}, f32[5,1280]{1,0:T(8,128)S(1)}, ...), condition=%wide.region_14.14_spmd.clone, body=%wide.region_13.13_spmd.clone.sunk | while | flops 1524421 | bytes 2295300 | solution.py:79
  1180.9 5.6 fusion.258
  1187.9 132.4 %while.80 = (s32[]{:T(128)}, f32[5,1280]{1,0:T(8,128)S(1)}, f32[5,1280]{1,0:T(8,128)S(1)}, f32[16,8,5,1280]{3,1,0,2:T(8,128)}, s32[16,8]{0,1:T(8,128)S(1)}, /*in...) while((s32[]{:T(128)}, f32[5,1280]{1,0:T(8,128)S(1)}, ...), condition=%wide.region_14.14_spmd.clone, body=%wide.region_13.13_spmd.clone.sunk | while | flops 1524421 | bytes 2295300 | solution.py:79
  1323.4 5.6 fusion.258
  1330.3 132.4 %while.80 = (s32[]{:T(128)}, f32[5,1280]{1,0:T(8,128)S(1)}, f32[5,1280]{1,0:T(8,128)S(1)}, f32[16,8,5,1280]{3,1,0,2:T(8,128)}, s32[16,8]{0,1:T(8,128)S(1)}, /*in...) while((s32[]{:T(128)}, f32[5,1280]{1,0:T(8,128)S(1)}, ...), condition=%wide.region_14.14_spmd.clone, body=%wide.region_13.13_spmd.clone.sunk | while | flops 1524421 | bytes 2295300 | solution.py:79
  1465.9 5.6 fusion.258
  1472.8 132.4 %while.80 = (s32[]{:T(128)}, f32[5,1280]{1,0:T(8,128)S(1)}, f32[5,1280]{1,0:T(8,128)S(1)}, f32[16,8,5,1280]{3,1,0,2:T(8,128)}, s32[16,8]{0,1:T(8,128)S(1)}, /*in...) while((s32[]{:T(128)}, f32[5,1280]{1,0:T(8,128)S(1)}, ...), condition=%wide.region_14.14_spmd.clone, body=%wide.region_13.13_spmd.clone.sunk | while | flops 1524421 | bytes 2295300 | solution.py:79
  1608.3 5.6 fusion.258
  1615.3 132.4 %while.80 = (s32[]{:T(128)}, f32[5,1280]{1,0:T(8,128)S(1)}, f32[5,1280]{1,0:T(8,128)S(1)}, f32[16,8,5,1280]{3,1,0,2:T(8,128)}, s32[16,8]{0,1:T(8,128)S(1)}, /*in...) while((s32[]{:T(128)}, f32[5,1280]{1,0:T(8,128)S(1)}, ...), condition=%wide.region_14.14_spmd.clone, body=%wide.region_13.13_spmd.clone.sunk | while | flops 1524421 | bytes 2295300 | solution.py:79
  1750.8 5.6 fusion.258
  1757.7 132.4 %while.80 = (s32[]{:T(128)}, f32[5,1280]{1,0:T(8,128)S(1)}, f32[5,1280]{1,0:T(8,128)S(1)}, f32[16,8,5,1280]{3,1,0,2:T(8,128)}, s32[16,8]{0,1:T(8,128)S(1)}, /*in...) while((s32[]{:T(128)}, f32[5,1280]{1,0:T(8,128)S(1)}, ...), condition=%wide.region_14.14_spmd.clone, body=%wide.region_13.13_spmd.clone.sunk | while | flops 1524421 | bytes 2295300 | solution.py:79
  1893.2 5.6 fusion.258
  (3598 shorter events, 1468.8 us)
Async XLA Ops:
  0.0 2.7 copy-start
  3.3 8.2 copy-start.1
  3.3 8.3 copy-start.2
  4.7 27.5 %all-to-all-start = ((bf16[8,3,8,4096]{3,2,1,0:T(8,128)(2,1)}), bf16[8,3,8,4096]{3,2,1,0:T(8,128)(2,1)S(1)}, u32[]{:S(2)}, u32[]{:S(2)}) async-start(bf16[8,3,8,4096]{3,2,1,0:T(8,128)(2,1)} %broadcast_select_fusion.1), calls=%async_computation | async-start | bytes 3145728 | tf_op jit(solution)/shard_map/all_to_all | solution.py:145
  66.9 24.8 %all-to-all-start.1 = ((f32[8,160,160]{2,0,1:T(8,128)}), f32[8,160,160]{2,0,1:T(8,128)S(1)}, u32[]{:S(2)}, u32[]{:S(2)}) async-start(f32[8,160,160]{2,0,1:T(8,128)} %copy.79), calls=%async_computation.1 | async-start | bytes 2621440 | tf_op jit(solution)/shard_map/all_to_all | solution.py:160
  268.5 24.5 %all-to-all-start.2 = ((f32[128,1,1600]{2,1,0:T(1,128)}), f32[128,1,1600]{2,1,0:T(1,128)S(1)}, u32[]{:S(2)}, u32[]{:S(2)}) async-start(f32[128,1,1600]{2,1,0:T(1,128)} %reshape.1094), calls=%async_computation.2 | async-start | bytes 1703936 | tf_op jit(solution)/shard_map/all_to_all | solution.py:170
where the time goes:
time: 1920 us; the launch traced here: 1900 us
  other arithmetic  1250 us (65%)
  local copies, waits for them, and re-layouts  345 us (18%)
  matrix products  208 us (11%)
  waiting for transfers between devices  54.3 us (3%)
  starting transfers between devices  20.7 us (1%)
    lt x176, other arithmetic, advance(): is_low = slot < low_length  862 us
    while x1232, other arithmetic  150 us
    dot_general x10, matrix products, one_columns(): return jnp.dot(flat_rows, dft_table(base), precision=highest)  136 us
    dynamic_update_slice x176, local copies, waits for them, and re-layouts, one_block(): state, table = lax.scan(advance, state, slots, unroll=8)  134 us
    sqrt x880, other arithmetic, advance(): jnp.sqrt(ratio)[:, None]  128 us
    slice x176, local copies, waits for them, and re-layouts, one_block(): state, table = lax.scan(advance, state, slots, unroll=8)  105 us
    dot_general x11, matrix products, one_block(): sums = jnp.einsum('sqhl,qhlc->qcs', both, scaled, precision=highest)  61.2 us
  transfers between devices with their start and end apart: 3, of which 3 were waited for; matrix products, arithmetic and copies ran while one was open for 0% of the time, Pallas kernels for 0%

commit v1 on v0

v1 whole, which is shorter than its diff:
```python
import math

import jax
import jax.numpy as jnp
import numpy as np
from jax import lax
from jax.experimental import pallas as pl
from jax.experimental.pallas import tpu as pltpu
from jax.sharding import PartitionSpec as P

NLON = 2560
NLAT = 1280
M = 1280
NEED = 12
MOST = 3
LEV = 8
PAIRS = 5
STEPS = 1296
CHUNK = 144
MIB = 2**20
F32 = jnp.float32
BF16 = jnp.bfloat16

EVENS = [(i, h, c) for i in range(5) for h in range(2) if (i + h) % 2 == 0 for c in range(2)]
ODDS = [(i, h, c) for i in range(5) for h in range(2) if (i + h) % 2 == 1 for c in range(2)]
SLOT = {e: 2 * w for w, e in enumerate(EVENS)} | {e: 2 * w + 1 for w, e in enumerate(ODDS)}


def dft_tables():
    s = np.arange(8)
    points = np.concatenate(
        [(s[:, None] * 160 + np.arange(128)).ravel(), (s[:, None] * 160 + np.arange(128, 160)).ravel()]
    )
    l2, t = np.meshgrid(np.arange(4), np.arange(16), indexing="ij")
    order = np.zeros((2, 10, 2, 64), np.int64)
    part = np.zeros((2, 10, 2, 64), np.int64)
    for q in range(2):
        for w in range(10):
            for half in range(2):
                i, h, c = (EVENS if q == half else ODDS)[w]
                pair = 5 * (t * 8 + 2 * l2 + half) + i
                order[q, w, half] = (pair if h == 0 else M - 1 - pair).ravel()
                part[q, w, half] = c
    order, part = order.reshape(2, 1, 1280), part.reshape(2, 1, 1280)
    angle = (points[None, :, None] * order % NLON) * (2.0 * np.pi / NLON)
    table = np.where(part == 0, np.cos(angle), -np.sin(angle)) / math.sqrt(NLON)
    high = table.astype(BF16)
    low = (table - high.astype(np.float64)).astype(BF16)
    return high, low


def latitudes():
    b, a2, l, t = np.meshgrid(np.arange(5), np.arange(2), np.arange(4), np.arange(16), indexing="ij")
    lat = (l * 160 + b * 32 + 2 * t + a2).reshape(5, 128)
    colat = np.pi * (lat + 0.75) / (NLAT + 0.5)
    return np.concatenate([colat, np.full((3, 128), np.pi / 2)])


def holder_of(owner_ref, need_ref, at):
    holder = owner_ref[need_ref[at]]
    device = (holder * 9363) >> 16
    return device & 7, holder - 7 * device


def pack_kernel(owner_ref, need_ref, me_ref, source_ref, out_ref, rows_ref, turned_ref):
    lane = lax.broadcasted_iota(jnp.int32, (32, 128), 1)
    for s in range(7):
        for i in range(32):
            rows_ref[pl.ds(i, 8, stride=32), :] = source_ref[s, :, i * 128 : (i + 1) * 128].astype(F32)
        for lp in range(4):
            one = rows_ref[lp * 64 : lp * 64 + 32, :]
            two = rows_ref[lp * 64 + 32 : lp * 64 + 64, :]
            top = jnp.where(lane < 64, one, pltpu.roll(two, 64, 1))
            low = jnp.where(lane < 64, pltpu.roll(one, 64, 1), two)
            at = slice(lp * 128, (lp + 1) * 128)
            turned_ref[s, 0:32, at] = top.astype(BF16)
            turned_ref[s, 32:64, at] = low.astype(BF16)
    me = me_ref[0]

    def one_dest(dest, _):
        def one_need(i, count):
            lat, slot = holder_of(owner_ref, need_ref, dest * NEED + i)

            @pl.when(lat == me)
            def _():
                out_ref[dest * MOST + jnp.minimum(count, MOST - 1)] = turned_ref[slot]

            return count + (lat == me).astype(jnp.int32)

        lax.fori_loop(0, NEED, one_need, jnp.int32(0))
        return 0

    lax.fori_loop(0, 8, one_dest, 0)


def regrid_kernel(
    owner_ref, need_ref, me_ref, pattern_ref, codes_ref, blocks_ref, cols_ref, rmat_ref, out_ref,
    left_ref, acc_ref, tail_ref, packed_ref, where_ref, seen_ref,
):
    me = me_ref[0]
    for l in range(8):
        seen_ref[l] = 0

    def locate(i, _):
        lat, _ = holder_of(owner_ref, need_ref, me * NEED + i)
        rank = seen_ref[lat]
        where_ref[i] = lat * MOST + jnp.minimum(rank, MOST - 1)
        seen_ref[lat] = rank + 1
        return 0

    lax.fori_loop(0, NEED, locate, 0)
    tail_ref[...] = jnp.zeros_like(tail_ref)
    lane = lax.broadcasted_iota(jnp.int32, (64, 128), 1)
    zero = jnp.zeros((64, 128), BF16)
    south = me >= 4

    for b in range(5):
        row_block = jnp.where(south, 4 - b, b)
        sums = [None, None]
        for k in range(4):
            term = row_block * 4 + k
            at = where_ref[pattern_ref[term]]
            odd = codes_ref[term] & 1

            @pl.when(odd == 0)
            def _():
                for lp in range(4):
                    tile = blocks_ref[at, :, lp * 128 : (lp + 1) * 128]
                    left_ref[lp * 128 : lp * 128 + 64, :] = jnp.where(lane < 64, tile, zero)
                    left_ref[lp * 128 + 64 : lp * 128 + 128, :] = jnp.where(lane < 64, zero, tile)

            @pl.when(odd == 1)
            def _():
                for lp in range(4):
                    tile = blocks_ref[at, :, lp * 128 : (lp + 1) * 128].astype(F32)
                    both = jnp.concatenate([tile, jnp.zeros((64, 128), F32)], axis=0)
                    left_ref[lp * 128 : (lp + 1) * 128, :] = both.T.astype(BF16)

            inner = jnp.dot(left_ref[...], cols_ref[term], preferred_element_type=F32).astype(BF16)
            for half in range(2):
                new = jnp.dot(
                    rmat_ref[term], inner[half * 256 : (half + 1) * 256], preferred_element_type=F32
                )
                sums[half] = new if k == 0 else sums[half] + new
        for half in range(2):
            acc_ref[half * 128 : (half + 1) * 128, :] = sums[half][:, :128]
            tail_ref[half * 128 : (half + 1) * 128, 0:32] = sums[half][:, 128:160]
        for t in range(16):
            main = [acc_ref[pl.ds(2 * t + a, 8, stride=32), :] for a in range(2)]
            out_ref[t, b * 16 : (b + 1) * 16, :] = jnp.concatenate(main, axis=0).astype(BF16)
            rest = jnp.concatenate([tail_ref[pl.ds(2 * t + a, 8, stride=32), :] for a in range(2)], axis=0)
            if b == 0:
                packed_ref[0, t] = rest
            elif b < 4:
                packed_ref[0, t] += pltpu.roll(rest, 32 * b, 1)
            else:
                packed_ref[1, t] = rest
    for t in range(16):
        out_ref[t, 80:96, :] = packed_ref[0, t].astype(BF16)
        out_ref[t, 96:112, :] = packed_ref[1, t].astype(BF16)


def dft_kernel(rows_ref, high_ref, low_ref, out_ref, both_ref, sums_ref, spread_ref):
    step = pl.program_id(0)
    lane = lax.broadcasted_iota(jnp.int32, (80, 128), 1)

    @pl.when(step == 0)
    def _():
        quarter = lax.broadcasted_iota(jnp.int32, (16, 128), 1) // 32
        sums_ref[1600:1664, :] = jnp.zeros((64, 128), F32)
        for q in range(2):

            def mixed(s, at):
                one, two = rows_ref[s, at, :].astype(F32), rows_ref[s + 8, at, :].astype(F32)
                return one + two if q == 0 else one - two

            def put(row, count, at, value):
                high = value.astype(BF16)
                both_ref[q, row : row + count, at] = high
                both_ref[q, 80 + row : 80 + row + count, at] = (value - high.astype(F32)).astype(BF16)

            for s in range(8):
                put(0, 80, slice(s * 128, (s + 1) * 128), mixed(s, slice(0, 80)))
            for group in range(2):
                first = [mixed(group * 4 + j, slice(80, 96)) for j in range(4)]
                last = [mixed(group * 4 + j, slice(96, 112)) for j in range(4)]
                for b in range(5):
                    value = jnp.zeros((16, 128), F32)
                    for j in range(4):
                        tile = first[j] if b < 4 else last[j]
                        shift = (32 * (j - (b if b < 4 else 0))) % 128
                        moved = tile if shift == 0 else pltpu.roll(tile, shift, 1)
                        value = jnp.where(quarter == j, moved, value)
                    put(b * 16, 16, slice(1024 + group * 128, 1152 + group * 128), value)

    outs = []
    for q in range(2):
        main = jnp.dot(both_ref[q], high_ref[q], preferred_element_type=F32)
        rest = jnp.dot(both_ref[q, 0:80, :], low_ref[q], preferred_element_type=F32)
        outs.append(main[0:80] + main[80:160] + rest)
    for half in range(2):
        at = slice(half * 128, (half + 1) * 128)
        even = jnp.where(lane < 64, outs[0][:, at], outs[1][:, at])
        odd = jnp.where(lane < 64, outs[1][:, at], outs[0][:, at])
        base = pl.multiple_of(step * 320 + half * 160, 16)
        sums_ref[pl.ds(base, 80), :] = even
        sums_ref[pl.ds(base + 80, 80), :] = odd

    @pl.when(step == pl.num_programs(0) - 1)
    def _():
        for k in range(13):
            turned = sums_ref[k * 128 : (k + 1) * 128, :].T
            for group in range(8):
                l = 2 * (group % 4) + group // 4
                spread_ref[pl.ds(l * 256 + k, 16, stride=16), :] = turned[group * 16 : (group + 1) * 16]
        for d in range(128):
            out_ref[d] = spread_ref[d * 16 : (d + 1) * 16, :].astype(BF16)


def table_kernel(coef_ref, switch_ref, cosine_ref, low_ref, start_ref, high_out, low_out, state_ref, rows_ref):
    step = pl.program_id(0)

    @pl.when(step == 0)
    def _():
        state_ref[...] = jnp.zeros_like(state_ref)

    cosine = cosine_ref[...]
    switches = [switch_ref[i] for i in range(PAIRS)]

    def sixteen(part, state):
        base = step * CHUNK + part * 16
        state = list(state)
        for k in range(16):
            slot = base + k
            for i in range(PAIRS):
                one, two = state[2 * i], state[2 * i + 1]
                grow = coef_ref[(2 * i) * STEPS + slot]
                back = coef_ref[(2 * i + 1) * STEPS + slot]
                value = (cosine * grow) * one - two * back
                if k == 0:
                    value = jnp.where(slot == 0, low_ref[i], value)
                value = jnp.where(slot == switches[i], start_ref[i], value)
                state[2 * i], state[2 * i + 1] = value, one
                rows_ref[i, k * 8 : (k + 1) * 8, :] = value
        at = pl.ds(pl.multiple_of(part * 16, 16), 16)
        for i in range(PAIRS):
            for b in range(5):
                value = rows_ref[i, pl.ds(b, 16, stride=8), :]
                high = value.astype(BF16)
                high_out[i, at, b * 128 : (b + 1) * 128] = high
                low_out[i, at, b * 128 : (b + 1) * 128] = (value - high.astype(F32)).astype(BF16)
        return tuple(state)

    state = lax.fori_loop(0, CHUNK // 16, sixteen, tuple(state_ref[j] for j in range(2 * PAIRS)))
    for j in range(2 * PAIRS):
        state_ref[j] = state[j]


def sums_kernel(first_ref, blocks_ref, high_ref, low_ref, out_ref, spread_ref, turned_ref, left_ref):
    step = pl.program_id(0)

    @pl.when(step == 0)
    def _():
        lane = lax.broadcasted_iota(jnp.int32, (8, 128), 1)
        for d in range(128):
            spread_ref[d * 16 : (d + 1) * 16, :] = blocks_ref[d].astype(F32)
        for k in range(13):
            parts = [spread_ref[pl.ds(l * 256 + k, 16, stride=16), :] for l in (0, 1, 2, 3, 7, 6, 5, 4)]
            turned_ref[k * 128 : (k + 1) * 128, :] = jnp.concatenate(parts, axis=0).T
        for i in range(PAIRS):
            for h in range(2):
                for b in range(5):
                    north, south = [], []
                    for c in range(2):
                        base = SLOT[(i, h, c)] * 80 + b * 16
                        one, two = turned_ref[base : base + 8, :], turned_ref[base + 8 : base + 16, :]
                        north.append(jnp.where(lane < 64, one, pltpu.roll(two, 64, 1)))
                        south.append(jnp.where(lane < 64, pltpu.roll(one, 64, 1), two))
                    at = slice(b * 128, (b + 1) * 128)
                    left_ref[i, h * 16 : h * 16 + 16, at] = jnp.concatenate(north, axis=0).astype(BF16)
                    left_ref[i, 32 + h * 16 : 48 + h * 16, at] = jnp.concatenate(south, axis=0).astype(BF16)

    left = left_ref[step]
    both_last = (((1,), (1,)), ((), ()))
    sums = lax.dot_general(left, high_ref[0], both_last, preferred_element_type=F32)
    sums += lax.dot_general(left, low_ref[0], both_last, preferred_element_type=F32)
    pair = first_ref[0] + step
    slot = lax.broadcasted_iota(jnp.int32, (16, STEPS), 1)
    low = sums[0:16] + jnp.where(slot & 1 == 0, sums[32:48], -sums[32:48])
    high = sums[16:32] + jnp.where((slot + pair) & 1 == 0, sums[48:64], -sums[48:64])
    result = jnp.where(slot < M - pair, low, high)
    out_ref[0] = result[:, : M + 1]


def vmem(shape=None, index=None):
    if shape is None:
        return pl.BlockSpec(memory_space=pltpu.VMEM)
    return pl.BlockSpec(shape, index)


SMEM = pl.BlockSpec(memory_space=pltpu.SMEM)


def params(limit):
    return pltpu.CompilerParams(vmem_limit_bytes=limit * MIB)


def cost(flops, moved):
    return pl.CostEstimate(flops=flops, bytes_accessed=moved, transcendentals=0)


def legendre_table(first):
    pair = first + jnp.arange(PAIRS, dtype=jnp.int32)
    slot = jnp.arange(STEPS, dtype=jnp.int32)[None, :]
    is_low = slot < (M - pair)[:, None]
    order = jnp.where(is_low, pair[:, None], M - 1 - pair[:, None])
    degree = jnp.where(is_low, pair[:, None] + slot, slot - 1)
    live = slot <= M
    grows = (degree > order) & live
    back = (degree - 1 > order) & live
    order_f, degree_f = order.astype(F32), degree.astype(F32)
    lower_f = degree_f - 1.0
    ratio = (4.0 * degree_f * degree_f - 1.0) / jnp.where(grows, degree_f * degree_f - order_f * order_f, 1.0)
    inverse = (lower_f * lower_f - order_f * order_f) / jnp.where(back, 4.0 * lower_f * lower_f - 1.0, 1.0)
    grow = jnp.where(grows, jnp.sqrt(jnp.where(grows, ratio, 1.0)), 0.0)
    keep = jnp.where(back, grow * jnp.sqrt(jnp.where(back, inverse, 1.0)), 0.0)
    coef = jnp.stack([grow, keep], axis=1).reshape(-1)

    terms = 0.5 * np.log1p(0.5 / np.arange(1, M, dtype=np.float64))
    logs = np.concatenate([np.zeros(1), np.cumsum(terms)]) + 0.5 * math.log(0.5)
    logs = jnp.asarray(logs.astype(np.float32))
    colat = latitudes()
    log_sine = jnp.asarray(np.log(np.sin(colat)).astype(np.float32))
    cosine = jnp.asarray(np.cos(colat).astype(np.float32))
    weight = jnp.asarray((np.pi * np.sin(colat) * math.sqrt(NLAT) / (NLAT + 0.5)).astype(np.float32))
    low_logs = lax.dynamic_slice(logs, (first,), (PAIRS,))
    high_logs = lax.dynamic_slice(logs, (M - PAIRS - first,), (PAIRS,))[::-1]

    def sectoral(picked, which):
        exponent = picked[:, None, None] + which.astype(F32)[:, None, None] * log_sine[None]
        ramp = jnp.clip((exponent + 75.0) / 10.0, 0.0, 1.0)
        return jnp.exp(jnp.maximum(exponent, -75.0)) * ramp * weight[None]

    low = sectoral(low_logs, pair)
    high = sectoral(high_logs, M - 1 - pair)
    shape = jax.ShapeDtypeStruct((PAIRS, STEPS, 640), BF16)
    block = vmem((PAIRS, CHUNK, 640), lambda g: (0, g, 0))
    return pl.pallas_call(
        table_kernel,
        grid=(STEPS // CHUNK,),
        out_shape=(shape, shape),
        in_specs=[SMEM, SMEM, vmem(), vmem(), vmem()],
        out_specs=(block, block),
        scratch_shapes=[pltpu.VMEM((2 * PAIRS, 8, 128), F32), pltpu.VMEM((PAIRS, 128, 128), F32)],
        compiler_params=params(16),
        cost_estimate=cost(60_000_000, 16_600_000),
        name="legendre_table",
    )(coef, M - pair, cosine, low, high)


def body(source, row_map, col_map, pattern, codes, need_list, owner):
    lat_me = lax.axis_index("lat").astype(jnp.int32)
    tile_me = lax.axis_index("tile").astype(jnp.int32)
    first = (tile_me * lax.axis_size("lat") + lat_me) * PAIRS
    me = lat_me.reshape(1)
    needs = need_list.reshape(-1)
    outgoing = pl.pallas_call(
        pack_kernel,
        out_shape=jax.ShapeDtypeStruct((8 * MOST, 64, 512), BF16),
        in_specs=[SMEM, SMEM, SMEM, vmem()],
        out_specs=vmem(),
        scratch_shapes=[pltpu.VMEM((256, 128), F32), pltpu.VMEM((7, 64, 512), BF16)],
        compiler_params=params(16),
        cost_estimate=cost(1_000_000, 2_000_000),
        name="pack",
    )(owner, needs, me, source)
    incoming = lax.all_to_all(outgoing, "lat", split_axis=0, concat_axis=0, tiled=True)

    high, low = legendre_table(first)

    code = codes.reshape(-1)
    odd = (code % 2 == 1)[:, None, None]
    rmap = row_map.reshape(20, 32, 64)
    rmap = jnp.where(((code == 1) | (code == 2))[:, None, None], rmap[:, :, ::-1], rmap)
    rmap = jnp.where(lat_me >= 4, rmap[:, ::-1, :], rmap)
    halves = jnp.swapaxes(rmap.reshape(20, 32, 32, 2), 2, 3).reshape(20, 32, 64)
    rmap = jnp.where(odd, rmap, halves)
    eye = jnp.eye(4, dtype=BF16)
    rmat = (eye[None, :, None, :, None] * rmap[:, None, :, None, :]).reshape(20, 128, 256)
    cmap = col_map.reshape(20, 64, 160)
    cmap = jnp.where(((code == 2) | (code == 3))[:, None, None], cmap[:, ::-1, :], cmap)
    halves = jnp.swapaxes(cmap.reshape(20, 32, 2, 160), 1, 2).reshape(20, 64, 160)
    cols = jnp.concatenate([jnp.where(odd, halves, cmap), jnp.where(odd, 0, cmap)], axis=1)

    field = pl.pallas_call(
        regrid_kernel,
        out_shape=jax.ShapeDtypeStruct((16, 112, 128), BF16),
        in_specs=[SMEM] * 5 + [vmem()] * 3,
        out_specs=vmem(),
        scratch_shapes=[
            pltpu.VMEM((512, 128), BF16),
            pltpu.VMEM((256, 128), F32),
            pltpu.VMEM((256, 128), F32),
            pltpu.VMEM((2, 16, 16, 128), F32),
            pltpu.SMEM((16,), jnp.int32),
            pltpu.SMEM((8,), jnp.int32),
        ],
        compiler_params=params(32),
        cost_estimate=cost(700_000_000, 5_000_000),
        name="regrid",
    )(owner, needs, me, pattern.reshape(-1), code, incoming, cols, rmat)
    rows = lax.all_to_all(field, "tile", split_axis=0, concat_axis=0, tiled=True)

    table_high, table_low = (jnp.asarray(t) for t in dft_tables())
    table = vmem((2, 1280, 256), lambda g: (0, 0, g))
    spectral = pl.pallas_call(
        dft_kernel,
        grid=(5,),
        out_shape=jax.ShapeDtypeStruct((128, 16, 128), BF16),
        in_specs=[vmem((16, 112, 128), lambda g: (0, 0, 0)), table, table],
        out_specs=vmem((128, 16, 128), lambda g: (0, 0, 0)),
        scratch_shapes=[
            pltpu.VMEM((2, 160, 1280), BF16),
            pltpu.VMEM((1664, 128), F32),
            pltpu.VMEM((2048, 128), F32),
        ],
        compiler_params=params(32),
        cost_estimate=cost(1_000_000_000, 14_000_000),
        name="dft",
    )(rows, table_high, table_low)
    arranged = lax.all_to_all(spectral, ("lat", "tile"), split_axis=0, concat_axis=0, tiled=True)

    part = vmem((1, STEPS, 640), lambda g: (g, 0, 0))
    return pl.pallas_call(
        sums_kernel,
        grid=(PAIRS,),
        out_shape=jax.ShapeDtypeStruct((PAIRS, 2 * LEV, M + 1), F32),
        in_specs=[SMEM, vmem((128, 16, 128), lambda g: (0, 0, 0)), part, part],
        out_specs=vmem((1, 2 * LEV, M + 1), lambda g: (g, 0, 0)),
        scratch_shapes=[
            pltpu.VMEM((2048, 128), F32),
            pltpu.VMEM((1664, 128), F32),
            pltpu.VMEM((PAIRS, 64, 640), BF16),
        ],
        compiler_params=params(32),
        cost_estimate=cost(2_000_000_000, 17_000_000),
        name="sums",
    )(first.reshape(1), arranged, high, low)


def solution(mesh):
    placed = (
        P(("tile", "lat"), None, None),
        P("lat", "tile", None, None, None),
        P("lat", None, None, "tile"),
        P("lat", "tile", None),
        P("lat", "tile", None),
        P("tile", None, None),
        P(),
    )
    return jax.shard_map(
        body, mesh=mesh, in_specs=placed, out_specs=P(("tile", "lat"), None, None), check_vma=False
    )
```

time: 1920 us -> 127 us (0.07); the launches traced: 1900 us -> 126 us
  other arithmetic: 1250 us -> 7.17 us
  local copies, waits for them, and re-layouts: 345 us -> 42.4 us
  matrix products: 208 us -> 0 us
  Pallas kernels: 0 us -> 45.7 us
  waiting for transfers between devices: 54.3 us -> 9.09 us
    lt x176 -> x0, other arithmetic: 862 us -> none  [advance(): is_low = slot < low_length]
    dot_general x26 -> x0, matrix products: 208 us -> none  [the longest x10 136 us: one_columns(): return jnp.dot(flat_rows, dft_table(base), precision=highest)]
    while x1232 -> x0, other arithmetic: 150 us -> none
    dynamic_update_slice x176 -> x0, local copies, waits for them, and re-layouts: 134 us -> none  [one_block(): state, table = lax.scan(advance, state, slots, unroll=8)]
    sqrt x880 -> x0, other arithmetic: 128 us -> none  [advance(): jnp.sqrt(ratio)[:, None]]
    slice x177 -> x0, local copies, waits for them, and re-layouts: 105 us -> none  [the longest x176 105 us: one_block(): state, table = lax.scan(advance, state, slots, unroll=8)]
    pallas_call x0 -> x5, Pallas kernels: none -> 45.7 us  [the longest x1 18.6 us: legendre_table(): pl.pallas_call(table_kernel, grid=(STEPS // CHUNK,), out_shape=(shape, sh...]
    concatenate x176 -> x1, other arithmetic: 33.7 us -> 0.25 us  [body(): jnp.concatenate([jnp.where(odd, halves, cmap), jnp.where(odd, 0, cmap)],...]
  transfers between devices with their start and end apart: 3 -> 3, of which waited for: 3 -> 1; matrix products, arithmetic and copies ran while one was open for 0% -> 20% of each run, Pallas kernels for 0% -> 15%
where the time goes in v1:
time: 127 us; the launch traced here: 126 us
  Pallas kernels  45.7 us (36%)
  local copies, waits for them, and re-layouts  42.4 us (33%)
  starting transfers between devices  21.3 us (17%)
  waiting for transfers between devices  9.09 us (7%)
  other arithmetic  7.17 us (6%)
    unnamed x59, local copies, waits for them, and re-layouts  23.4 us
    pallas_call x1, Pallas kernels, legendre_table(): pl.pallas_call(table_kernel, grid=(STEPS // CHUNK,), out_shape=(shape, sh...  18.6 us
    pallas_call x1, Pallas kernels, body(): pl.pallas_call(regrid_kernel, out_shape=jax.ShapeDtypeStruct((16, 112, 12...  10.5 us
    mul x4, local copies, waits for them, and re-layouts, body(): eye[None, :, None, :, None] * rmap[:, None, :, None, :]  9.32 us
    all_to_all x1, waiting for transfers between devices, body(): lax.all_to_all(field, 'tile', split_axis=0, concat_axis=0, tiled=True)  9.08 us
    all_to_all x1, starting transfers between devices, body(): lax.all_to_all(spectral, ('lat', 'tile'), split_axis=0, concat_axis=0, ti...  7.78 us
    all_to_all x1, starting transfers between devices, body(): lax.all_to_all(outgoing, 'lat', split_axis=0, concat_axis=0, tiled=True)  6.95 us
    pallas_call x1, Pallas kernels, body(): pl.pallas_call(sums_kernel, grid=(PAIRS,), out_shape=jax.ShapeDtypeStruct...  6.65 us
  transfers between devices with their start and end apart: 3, of which 1 were waited for; matrix products, arithmetic and copies ran while one was open for 20% of the time, Pallas kernels for 15%

profile of v1, /device:TPU:1, one launch (start us, length us, event | category | flops | bytes accessed | tf_op | source)
XLA Modules:
  0.0 125.9 jit_solution(5989516904841633782)
XLA Ops:
  0.0 0.8 reshape.477.need_ref
  0.8 1.0 copy-done.7
  1.8 0.7 copy-done.8
  2.5 4.6 %pack.1 = bf16[24,64,512]{2,1,0:T(8,128)(2,1)} custom-call(s32[896]{0:T(1024)S(1)} %copy-done.8, s32[96]{0:T(128)S(1)} %reshape.477.need_ref, s32[1]{0:T(128)} %bitcast.1.me_ref, bf16[7,8,4096]{2,1,0:T(8,128)(2,1)S(1)} %copy-done.7), custom_call_target="tpu_custom_call" | custom-call | flops 1000000 | bytes 2000000 | tf_op jit(solution)/shard_map/pack/pallas_call | solution.py:367
  7.0 6.9 %all-to-all-start = ((bf16[24,64,512]{2,1,0:T(8,128)(2,1)}), bf16[24,64,512]{2,1,0:T(8,128)(2,1)S(1)}, u32[]{:S(2)}, u32[]{:S(2)}) async-start(bf16[24,64,512]{2,1,0:T(8,128)(2,1)} %pack.1), calls=%async_computation | async-start | bytes 3145728 | tf_op jit(solution)/shard_map/all_to_all | solution.py:377
  14.0 1.4 %fusion.12 = (f32[5]{0:T(128)S(1)}, f32[5]{0:T(128)}) fusion(f32[1280]{0:T(1024)} %constant.84.clone, s32[]{:T(128)S(6)} %select_n.163, s32[]{:T(128)S(6)} %select_n.162), kind=kLoop, calls=%fused_computation.43 | loop fusion | bytes 88 | tf_op jit(solution)/shard_map/dynamic_slice | solution.py:337
  15.4 0.7 rev.15
  16.0 0.0 copy-done.22
  16.0 0.1 copy.23
  16.1 0.1 reshape.479.pattern_ref
  16.2 0.1 copy.24
  16.3 0.1 reshape.480.codes_ref
  16.4 0.5 compare_or_fusion
  16.9 0.1 mul.169
  17.0 0.8 mul.170
  17.8 0.0 copy-done.14
  17.8 0.2 copy.26
  18.0 0.7 rev.13
  18.6 0.1 broadcast_select_fusion.2
  18.8 0.8 rev.14
  19.6 0.0 copy-start.12
  19.6 0.1 copy.30
  19.7 0.1 bitcast_select_fusion.1
  19.8 0.8 copy.29
  20.6 0.0 copy-done.12
  20.7 1.9 %rev.12 = bf16[20,64,160]{2,1,0:T(8,128)(2,1)} reverse(bf16[20,64,160]{2,1,0:T(8,128)(2,1)S(1)} %bitcast.22), dimensions={1} | reverse | bytes 819200 | tf_op jit(solution)/shard_map/rev | solution.py:391
  22.5 1.3 broadcast_select_fusion.1
  23.8 1.2 reshape.482
  25.0 1.2 copy.25
  26.2 3.6 %mul.172 = bf16[20,4,32,4,64]{4,3,2,1,0:T(4,128)(2,1)} broadcast(bf16[20,32,64]{2,1,0:T(8,128)(2,1)} %copy.29), dimensions={0,2,4} | broadcast | bytes 1392640 | tf_op jit(solution)/shard_map/mul | solution.py:389
  29.8 4.8 %mul.173 = bf16[20,128,256]{2,1,0:T(8,128)(2,1)} reshape(bf16[20,4,32,4,64]{4,3,2,1,0:T(4,128)(2,1)} %mul.172) | data formatting | bytes 2621440 | tf_op jit(solution)/shard_map/mul | solution.py:389
  34.6 0.6 broadcast_subtract_fusion.1
  35.2 0.6 iota_add_fusion.1
  35.8 0.6 iota_compare_fusion
  36.4 0.6 iota_add_fusion
  37.0 0.8 bitcast_select_fusion
  37.8 0.0 copy-start.11
  37.8 0.0 copy-start.13
  37.8 0.2 pad_maximum_fusion.cols_ref
  38.0 1.0 copy-done.11
  39.1 1.2 broadcast_multiply_fusion.rmat_ref
  40.3 0.0 all-to-all-done.blocks_ref
  40.3 0.0 copy-done.9
  40.3 1.3 %copy-done.6 = bf16[20,128,256]{2,1,0:T(8,128)(2,1)S(1)} copy-done((bf16[20,128,256]{2,1,0:T(8,128)(2,1)S(1)}, bf16[20,128,256]{2,1,0:T(8,128)(2,1)}, u32[]{:S(2)}) %copy-start.6) | copy-done | bytes 1310744
  41.6 10.5 %regrid.1 = bf16[16,112,128]{2,1,0:T(8,128)(2,1)} custom-call(s32[896]{0:T(1024)S(1)} %copy-done.9, s32[96]{0:T(128)S(1)} %reshape.477.need_ref, s32[1]{0:T(128)} %bitcast.1.me_ref, s32[20]{0:T(128)S(1)} %reshape.479.pattern_ref, s32[20]{0:T(128)S(1)} %reshape.480.codes_ref, bf16[24,64,512]{2,1,0:T(8,128)(2,1)S(1)} %all-to-all-done.blocks_ref, ...), custom_call_target="tpu_custom_call" | custom-call | flops 700000000 | bytes 5000000 | tf_op jit(solution)/shard_map/regrid/pallas_call | solution.py:395
  52.1 6.6 %all-to-all-start.1 = ((bf16[16,112,128]{2,1,0:T(8,128)(2,1)}), bf16[16,112,128]{2,1,0:T(8,128)(2,1)S(1)}, u32[]{:S(2)}, u32[]{:S(2)}) async-start(bf16[16,112,128]{2,1,0:T(8,128)(2,1)} %regrid.1), calls=%async_computation.1 | async-start | bytes 917504 | tf_op jit(solution)/shard_map/all_to_all | solution.py:412
  58.7 0.5 multiply_select_fusion
  59.2 9.1 %all-to-all-done.1.rows_ref = bf16[16,112,128]{2,1,0:T(8,128)(2,1)S(1)} async-done(((bf16[16,112,128]{2,1,0:T(8,128)(2,1)}), bf16[16,112,128]{2,1,0:T(8,128)(2,1)S(1)}, u32[]{:S(2)}, u32[]{:S(2)}) %all-to-all-start.1) | async-done | bytes 458784 | tf_op jit(solution)/shard_map/all_to_all | solution.py:412
  68.3 2.9 %copy-done.4 = bf16[2,1280,1280]{2,1,0:T(8,128)(2,1)S(1)} copy-done((bf16[2,1280,1280]{2,1,0:T(8,128)(2,1)S(1)}, bf16[2,1280,1280]{2,1,0:T(8,128)(2,1)}, u32[]{:S(2)}) %copy-start.4) | copy-done | bytes 6553624
  71.2 2.9 %copy-done.5 = bf16[2,1280,1280]{2,1,0:T(8,128)(2,1)S(1)} copy-done((bf16[2,1280,1280]{2,1,0:T(8,128)(2,1)S(1)}, bf16[2,1280,1280]{2,1,0:T(8,128)(2,1)}, u32[]{:S(2)}) %copy-start.5) | copy-done | bytes 6553624
  74.0 0.0 copy-start.10
  74.0 5.3 %dft.1 = bf16[128,16,128]{2,1,0:T(8,128)(2,1)} custom-call(bf16[16,112,128]{2,1,0:T(8,128)(2,1)S(1)} %all-to-all-done.1.rows_ref, bf16[2,1280,1280]{2,1,0:T(8,128)(2,1)S(1)} %copy-done.5, bf16[2,1280,1280]{2,1,0:T(8,128)(2,1)S(1)} %copy-done.4), custom_call_target="tpu_custom_call" | custom-call | flops 1000000000 | bytes 14000000 | tf_op jit(solution)/shard_map/dft/pallas_call | solution.py:416
  79.4 7.8 %all-to-all-start.2 = ((bf16[128,16,128]{2,1,0:T(8,128)(2,1)}), bf16[128,16,128]{2,1,0:T(8,128)(2,1)S(1)}, u32[]{:S(2)}, u32[]{:S(2)}) async-start(bf16[128,16,128]{2,1,0:T(8,128)(2,1)} %dft.1), calls=%async_computation.2 | async-start | bytes 1048576 | tf_op jit(solution)/shard_map/all_to_all | solution.py:431
  87.2 0.1 pad_maximum_fusion.1
  87.2 0.1 reshape.487.coef_ref
  87.4 0.1 multiply_multiply_fusion.2
  87.5 18.6 %legendre_table.1 = (bf16[5,1296,640]{2,1,0:T(8,128)(2,1)S(1)}, bf16[5,1296,640]{2,1,0:T(8,128)(2,1)S(1)}) custom-call(f32[12960]{0:T(1024)S(1)} %reshape.487.coef_ref, s32[5]{0:T(128)S(1)} %get-tuple-element.22.switch_ref, f32[8,128]{1,0:T(8,128)S(1)} %copy-done.10, f32[5,8,128]{2,1,0:T(8,128)S(1)} %get-tuple-element.14.low_ref, ...), custom_call_target="tpu_custom_call" | custom-call | flops 60000000 | bytes 16600000 | tf_op jit(solution)/shard_map/legendre_table/pallas_call | solution.py:348
  106.1 0.0 copy-start
  106.1 3.2 %copy-done = bf16[5,1296,640]{2,1,0:T(8,128)(2,1)} copy-done((bf16[5,1296,640]{2,1,0:T(8,128)(2,1)}, bf16[5,1296,640]{2,1,0:T(8,128)(2,1)S(1)}, u32[]{:S(2)}) %copy-start) | copy-done | bytes 8294424
  109.4 3.2 %copy-done.2 = bf16[5,1296,640]{2,1,0:T(8,128)(2,1)} copy-done((bf16[5,1296,640]{2,1,0:T(8,128)(2,1)}, bf16[5,1296,640]{2,1,0:T(8,128)(2,1)S(1)}, u32[]{:S(2)}) %copy-start.2) | copy-done | bytes 8294424
  112.6 0.0 all-to-all-done.2.blocks_ref
  112.6 3.4 %copy-done.1 = bf16[5,1296,640]{2,1,0:T(8,128)(2,1)S(1)} copy-done((bf16[5,1296,640]{2,1,0:T(8,128)(2,1)S(1)}, bf16[5,1296,640]{2,1,0:T(8,128)(2,1)}, u32[]{:S(2)}) %copy-start.1) | copy-done | bytes 8294424
  115.9 3.4 %copy-done.3 = bf16[5,1296,640]{2,1,0:T(8,128)(2,1)S(1)} copy-done((bf16[5,1296,640]{2,1,0:T(8,128)(2,1)S(1)}, bf16[5,1296,640]{2,1,0:T(8,128)(2,1)}, u32[]{:S(2)}) %copy-start.3) | copy-done | bytes 8294424
  119.3 6.7 %sums.1 = f32[5,16,1281]{2,1,0:T(8,128)} custom-call(s32[1]{0:T(128)} %bitcast.first_ref, bf16[128,16,128]{2,1,0:T(8,128)(2,1)S(1)} %all-to-all-done.2.blocks_ref, bf16[5,1296,640]{2,1,0:T(8,128)(2,1)S(1)} %copy-done.1, bf16[5,1296,640]{2,1,0:T(8,128)(2,1)S(1)} %copy-done.3), custom_call_target="tpu_custom_call" | custom-call | flops 2000000000 | bytes 17000000 | tf_op jit(solution)/shard_map/sums/pallas_call | solution.py:434
  (40 shorter events, 0.1 us)
Async XLA Ops:
  0.8 1.0 copy-start.7
  1.8 0.7 copy-start.8
  7.0 9.0 %copy-start.22 = (s32[5,1,4]{0,2,1:T(4,128)S(1)}, s32[5,1,4]{0,2,1:T(4,128)}, u32[]{:S(2)}) copy-start(s32[5,1,4]{0,2,1:T(4,128)} %param.16) | copy-start | bytes 244
  7.0 9.2 %copy-start.23 = (s32[5,1,4]{0,2,1:T(4,128)S(1)}, s32[5,1,4]{0,2,1:T(4,128)}, u32[]{:S(2)}) copy-start(s32[5,1,4]{0,2,1:T(4,128)} %param.17) | copy-start | bytes 244
  7.0 10.7 %copy-start.14 = (bf16[5,1,4,32,64]{4,3,2,1,0:T(8,128)(2,1)S(1)}, bf16[5,1,4,32,64]{4,3,2,1,0:T(8,128)(2,1)}, u32[]{:S(2)}) copy-start(bf16[5,1,4,32,64]{4,3,2,1,0:T(8,128)(2,1)} %param.14) | copy-start | bytes 245764
  7.0 33.2 %all-to-all-start = ((bf16[24,64,512]{2,1,0:T(8,128)(2,1)}), bf16[24,64,512]{2,1,0:T(8,128)(2,1)S(1)}, u32[]{:S(2)}, u32[]{:S(2)}) async-start(bf16[24,64,512]{2,1,0:T(8,128)(2,1)} %pack.1), calls=%async_computation | async-start | bytes 3145728 | tf_op jit(solution)/shard_map/all_to_all | solution.py:377
  16.9 2.8 %copy-start.16 = (pred[20]{0:T(512)(128)(4,1)}, pred[20]{0:T(512)(128)(4,1)S(1)}, u32[]{:S(2)}) copy-start(pred[20]{0:T(512)(128)(4,1)S(1)} %get-tuple-element.19) | copy-start | bytes 64
  19.6 1.1 copy-start.12
  19.8 2.7 %copy-start.17 = (pred[20]{0:T(512)(128)(4,1)S(1)}, pred[20]{0:T(512)(128)(4,1)}, u32[]{:S(2)}) copy-start(pred[20]{0:T(512)(128)(4,1)} %copy-done.16) | copy-start | bytes 64
  37.8 1.3 %copy-start.11 = (bf16[20,128,256]{2,1,0:T(8,128)(2,1)S(1)}, bf16[20,128,256]{2,1,0:T(8,128)(2,1)}, u32[]{:S(2)}) copy-start(bf16[20,128,256]{2,1,0:T(8,128)(2,1)} %mul.173) | copy-start | bytes 3932164
  37.8 1.3 %copy-start.13 = (bf16[128,256]{1,0:T(8,128)(2,1)S(1)}, bf16[128,256]{1,0:T(8,128)(2,1)}, u32[]{:S(2)}) copy-start(bf16[128,256]{1,0:T(8,128)(2,1)} %mul.170) | copy-start | bytes 196612
  39.1 1.2 copy-start.9
  40.3 1.3 %copy-start.6 = (bf16[20,128,256]{2,1,0:T(8,128)(2,1)S(1)}, bf16[20,128,256]{2,1,0:T(8,128)(2,1)}, u32[]{:S(2)}) copy-start(bf16[20,128,256]{2,1,0:T(8,128)(2,1)} %broadcast_multiply_fusion.rmat_ref) | copy-start | bytes 3932164
  41.6 17.1 %copy-start.15 = (s32[1296]{0:T(1024)S(1)}, s32[1296]{0:T(1024)}, u32[]{:S(2)}) copy-start(s32[1296]{0:T(1024)} %iota_add_fusion) | copy-start | bytes 15556
  41.6 17.1 %copy-start.18 = (pred[1296]{0:T(1024)(128)(4,1)S(1)}, pred[1296]{0:T(1024)(128)(4,1)}, u32[]{:S(2)}) copy-start(pred[1296]{0:T(1024)(128)(4,1)} %iota_compare_fusion) | copy-start | bytes 3892
  41.6 17.1 %copy-start.26 = (s32[5]{0:T(128)S(1)}, s32[5]{0:T(128)}, u32[]{:S(2)}) copy-start(s32[5]{0:T(128)} %get-tuple-element.20) | copy-start | bytes 64
  41.6 17.1 %copy-start.27 = (s32[5]{0:T(128)S(1)}, s32[5]{0:T(128)}, u32[]{:S(2)}) copy-start(s32[5]{0:T(128)} %get-tuple-element.21) | copy-start | bytes 64
  52.1 16.2 %all-to-all-start.1 = ((bf16[16,112,128]{2,1,0:T(8,128)(2,1)}), bf16[16,112,128]{2,1,0:T(8,128)(2,1)S(1)}, u32[]{:S(2)}, u32[]{:S(2)}) async-start(bf16[16,112,128]{2,1,0:T(8,128)(2,1)} %regrid.1), calls=%async_computation.1 | async-start | bytes 917504 | tf_op jit(solution)/shard_map/all_to_all | solution.py:412
  68.3 2.9 %copy-start.4 = (bf16[2,1280,1280]{2,1,0:T(8,128)(2,1)S(1)}, bf16[2,1280,1280]{2,1,0:T(8,128)(2,1)}, u32[]{:S(2)}) copy-start(bf16[2,1280,1280]{2,1,0:T(8,128)(2,1)} %constant.89.clone.low_ref) | copy-start | bytes 19660804
  71.1 2.9 %copy-start.5 = (bf16[2,1280,1280]{2,1,0:T(8,128)(2,1)S(1)}, bf16[2,1280,1280]{2,1,0:T(8,128)(2,1)}, u32[]{:S(2)}) copy-start(bf16[2,1280,1280]{2,1,0:T(8,128)(2,1)} %constant.88.clone.high_ref) | copy-start | bytes 19660804
  74.0 13.4 %copy-start.19 = (f32[8,128]{1,0:T(8,128)S(1)}, f32[8,128]{1,0:T(8,128)}, u32[]{:S(2)}) copy-start(f32[8,128]{1,0:T(8,128)} %constant.87.clone) | copy-start | bytes 12292
  74.0 13.4 %copy-start.20 = (f32[8,128]{1,0:T(8,128)S(1)}, f32[8,128]{1,0:T(8,128)}, u32[]{:S(2)}) copy-start(f32[8,128]{1,0:T(8,128)} %constant.85.clone) | copy-start | bytes 12292
  74.0 13.4 %copy-start.21 = (f32[5]{0:T(128)S(1)}, f32[5]{0:T(128)}, u32[]{:S(2)}) copy-start(f32[5]{0:T(128)} %get-tuple-element.16) | copy-start | bytes 64
  74.0 13.4 %copy-start.24 = (f32[5]{0:T(128)S(1)}, f32[5]{0:T(128)}, u32[]{:S(2)}) copy-start(f32[5]{0:T(128)} %rev.15) | copy-start | bytes 64
  74.0 13.4 %copy-start.25 = (f32[5]{0:T(128)S(1)}, f32[5]{0:T(128)}, u32[]{:S(2)}) copy-start(f32[5]{0:T(128)} %get-tuple-element.23) | copy-start | bytes 64
  74.0 13.5 %copy-start.10 = (f32[8,128]{1,0:T(8,128)S(1)}, f32[8,128]{1,0:T(8,128)}, u32[]{:S(2)}) copy-start(f32[8,128]{1,0:T(8,128)} %constant.86.clone.cosine_ref) | copy-start | bytes 12292
  79.4 33.2 %all-to-all-start.2 = ((bf16[128,16,128]{2,1,0:T(8,128)(2,1)}), bf16[128,16,128]{2,1,0:T(8,128)(2,1)S(1)}, u32[]{:S(2)}, u32[]{:S(2)}) async-start(bf16[128,16,128]{2,1,0:T(8,128)(2,1)} %dft.1), calls=%async_computation.2 | async-start | bytes 1048576 | tf_op jit(solution)/shard_map/all_to_all | solution.py:431
  106.1 3.2 %copy-start = (bf16[5,1296,640]{2,1,0:T(8,128)(2,1)}, bf16[5,1296,640]{2,1,0:T(8,128)(2,1)S(1)}, u32[]{:S(2)}) copy-start(bf16[5,1296,640]{2,1,0:T(8,128)(2,1)S(1)} %get-tuple-element.7.high_ref) | copy-start | bytes 24883204
  109.4 3.2 %copy-start.2 = (bf16[5,1296,640]{2,1,0:T(8,128)(2,1)}, bf16[5,1296,640]{2,1,0:T(8,128)(2,1)S(1)}, u32[]{:S(2)}) copy-start(bf16[5,1296,640]{2,1,0:T(8,128)(2,1)S(1)} %get-tuple-element.8.low_ref) | copy-start | bytes 24883204
  112.6 3.4 %copy-start.1 = (bf16[5,1296,640]{2,1,0:T(8,128)(2,1)S(1)}, bf16[5,1296,640]{2,1,0:T(8,128)(2,1)}, u32[]{:S(2)}) copy-start(bf16[5,1296,640]{2,1,0:T(8,128)(2,1)} %copy-done) | copy-start | bytes 24883204
  115.9 3.4 %copy-start.3 = (bf16[5,1296,640]{2,1,0:T(8,128)(2,1)S(1)}, bf16[5,1296,640]{2,1,0:T(8,128)(2,1)}, u32[]{:S(2)}) copy-start(bf16[5,1296,640]{2,1,0:T(8,128)(2,1)} %copy-done.2) | copy-start | bytes 24883204

commit v2 on v1

v2 whole, which is shorter than its diff:
```python
import math

import jax
import jax.numpy as jnp
import numpy as np
from jax import lax
from jax.experimental import pallas as pl
from jax.experimental.pallas import tpu as pltpu
from jax.sharding import PartitionSpec as P

NLON = 2560
NLAT = 1280
M = 1280
NEED = 12
MOST = 3
LEV = 8
PAIRS = 5
STEPS = 1296
CHUNK = 144
MIB = 2**20
F32 = jnp.float32
BF16 = jnp.bfloat16

EVENS = [(i, h, c) for i in range(5) for h in range(2) if (i + h) % 2 == 0 for c in range(2)]
ODDS = [(i, h, c) for i in range(5) for h in range(2) if (i + h) % 2 == 1 for c in range(2)]
SLOT = {e: 2 * w for w, e in enumerate(EVENS)} | {e: 2 * w + 1 for w, e in enumerate(ODDS)}


def dft_tables():
    s = np.arange(8)
    points = np.concatenate(
        [(s[:, None] * 160 + np.arange(128)).ravel(), (s[:, None] * 160 + np.arange(128, 160)).ravel()]
    )
    l2, t = np.meshgrid(np.arange(4), np.arange(16), indexing="ij")
    order = np.zeros((2, 10, 2, 64), np.int64)
    part = np.zeros((2, 10, 2, 64), np.int64)
    for q in range(2):
        for w in range(10):
            for half in range(2):
                i, h, c = (EVENS if q == half else ODDS)[w]
                pair = 5 * (t * 8 + 2 * l2 + half) + i
                order[q, w, half] = (pair if h == 0 else M - 1 - pair).ravel()
                part[q, w, half] = c
    order, part = order.reshape(2, 1, 1280), part.reshape(2, 1, 1280)
    angle = (points[None, :, None] * order % NLON) * (2.0 * np.pi / NLON)
    table = np.where(part == 0, np.cos(angle), -np.sin(angle)) / math.sqrt(NLON)
    high = table.astype(BF16)
    low = (table - high.astype(np.float64)).astype(BF16)
    return [np.ascontiguousarray(x.reshape(2, 1280, 5, 256).transpose(2, 0, 1, 3)) for x in (high, low)]


def latitudes():
    b, a2, l, t = np.meshgrid(np.arange(5), np.arange(2), np.arange(4), np.arange(16), indexing="ij")
    lat = (l * 160 + b * 32 + 2 * t + a2).reshape(5, 128)
    colat = np.pi * (lat + 0.75) / (NLAT + 0.5)
    return np.concatenate([colat, np.full((3, 128), np.pi / 2)])


def holder_of(owner_ref, need_ref, dest, i):
    holder = owner_ref[need_ref[dest, i]]
    device = (holder * 9363) >> 16
    return device & 7, holder - 7 * device


def pack_kernel(owner_ref, need_ref, me_ref, source_hbm, out_ref, source_ref, rows_ref, turned_ref, list_ref, sems):
    loads = [pltpu.make_async_copy(source_hbm.at[s], source_ref.at[s], sems.at[s]) for s in range(7)]
    for load in loads:
        load.start()
    lane = lax.broadcasted_iota(jnp.int32, (32, 128), 1)
    me = me_ref[0]
    for at in range(8 * MOST):
        list_ref[at] = 0
    for dest in range(8):
        count = jnp.int32(0)
        for i in range(NEED):
            lat, slot = holder_of(owner_ref, need_ref, dest, i)
            hit = lat == me
            list_ref[jnp.where(hit, dest * MOST + jnp.minimum(count, MOST - 1), 8 * MOST)] = slot
            count = count + hit.astype(jnp.int32)
    for s in range(7):
        loads[s].wait()
        for i in range(32):
            rows_ref[s % 2, pl.ds(i, 8, stride=32), :] = source_ref[s, :, i * 128 : (i + 1) * 128].astype(F32)
        for lp in range(4):
            one = rows_ref[s % 2, lp * 64 : lp * 64 + 32, :]
            two = rows_ref[s % 2, lp * 64 + 32 : lp * 64 + 64, :]
            top = jnp.where(lane < 64, one, pltpu.roll(two, 64, 1))
            low = jnp.where(lane < 64, pltpu.roll(one, 64, 1), two)
            at = slice(lp * 128, (lp + 1) * 128)
            turned_ref[s, 0:32, at] = top.astype(BF16)
            turned_ref[s, 32:64, at] = low.astype(BF16)
    for at in range(8 * MOST):
        out_ref[at] = turned_ref[list_ref[at]]


def regrid_kernel(
    owner_ref, need_ref, me_ref, pattern_ref, codes_ref, blocks_hbm, cols_hbm, rmat_hbm, out_ref,
    blocks_ref, cols_ref, rmat_ref, sems, forms_ref, acc_ref, tail_ref, packed_ref, seen_ref,
):
    me = me_ref[0]
    maps = [
        pltpu.make_async_copy(cols_hbm, cols_ref, sems.at[NEED]),
        pltpu.make_async_copy(rmat_hbm, rmat_ref, sems.at[NEED + 1]),
    ]
    for l in range(8):
        seen_ref[l] = 0
    tail_ref[...] = jnp.zeros_like(tail_ref)
    lane = lax.broadcasted_iota(jnp.int32, (64, 128), 1)
    zero = jnp.zeros((64, 128), BF16)
    empty = jnp.zeros((64, 128), F32)
    south = me >= 4

    loads = []
    for i in range(NEED):
        lat, _ = holder_of(owner_ref, need_ref, me, i)
        rank = seen_ref[lat]
        at = lat * MOST + jnp.minimum(rank, MOST - 1)
        seen_ref[lat] = rank + 1
        loads.append(pltpu.make_async_copy(blocks_hbm.at[at], blocks_ref.at[i], sems.at[i]))
        loads[i].start()
    for move in maps:
        move.start()
    for i in range(NEED):
        loads[i].wait()
        for lp in range(4):
            tile = blocks_ref[i, :, lp * 128 : (lp + 1) * 128]
            forms_ref[2 * i, lp * 128 : lp * 128 + 64, :] = jnp.where(lane < 64, tile, zero)
            forms_ref[2 * i, lp * 128 + 64 : lp * 128 + 128, :] = jnp.where(lane < 64, zero, tile)
            both = jnp.concatenate([tile.astype(F32), empty], axis=0)
            forms_ref[2 * i + 1, lp * 128 : (lp + 1) * 128, :] = both.T.astype(BF16)

    for move in maps:
        move.wait()
    for b in range(5):
        row_block = jnp.where(south, 4 - b, b)
        sums = [None, None]
        for k in range(4):
            term = row_block * 4 + k
            form = forms_ref[pattern_ref[0, k, row_block] * 2 + (codes_ref[0, k, row_block] & 1)]
            inner = jnp.dot(form, cols_ref[term], preferred_element_type=F32).astype(BF16)
            for half in range(2):
                new = jnp.dot(
                    rmat_ref[term], inner[half * 256 : (half + 1) * 256], preferred_element_type=F32
                )
                sums[half] = new if k == 0 else sums[half] + new
        for half in range(2):
            acc_ref[b % 2, half * 128 : (half + 1) * 128, :] = sums[half][:, :128]
            tail_ref[b % 2, half * 128 : (half + 1) * 128, 0:32] = sums[half][:, 128:160]
        for t in range(16):
            at = [jnp.where(south, 31 - (2 * t + a), 2 * t + a) for a in range(2)]
            main = [acc_ref[b % 2, pl.ds(at[a], 8, stride=32), :] for a in range(2)]
            out_ref[t, b * 16 : (b + 1) * 16, :] = jnp.concatenate(main, axis=0).astype(BF16)
            rest = jnp.concatenate([tail_ref[b % 2, pl.ds(at[a], 8, stride=32), :] for a in range(2)], axis=0)
            if b == 0:
                packed_ref[t] = rest
            elif b < 4:
                packed_ref[t] += pltpu.roll(rest, 32 * b, 1)
            else:
                out_ref[t, 96:112, :] = rest.astype(BF16)
    for t in range(16):
        out_ref[t, 80:96, :] = packed_ref[t].astype(BF16)


def dft_kernel(rows_ref, high_hbm, low_hbm, out_ref, high_ref, low_ref, sems, both_ref, sums_ref, spread_ref):
    step = pl.program_id(0)
    lane = lax.broadcasted_iota(jnp.int32, (80, 128), 1)

    def load(g):
        return (
            pltpu.make_async_copy(high_hbm.at[g], high_ref.at[g], sems.at[g]),
            pltpu.make_async_copy(low_hbm.at[g], low_ref.at[g], sems.at[5 + g]),
        )

    @pl.when(step == 0)
    def _():
        for g in range(5):
            for move in load(g):
                move.start()
        quarter = lax.broadcasted_iota(jnp.int32, (16, 128), 1) // 32
        sums_ref[1600:1664, :] = jnp.zeros((64, 128), F32)
        for q in range(2):

            def mixed(s, at):
                one, two = rows_ref[s, at, :].astype(F32), rows_ref[s + 8, at, :].astype(F32)
                return one + two if q == 0 else one - two

            def put(row, count, at, value):
                high = value.astype(BF16)
                both_ref[q, row : row + count, at] = high
                both_ref[q, 80 + row : 80 + row + count, at] = (value - high.astype(F32)).astype(BF16)

            for s in range(8):
                put(0, 80, slice(s * 128, (s + 1) * 128), mixed(s, slice(0, 80)))
            for group in range(2):
                first = [mixed(group * 4 + j, slice(80, 96)) for j in range(4)]
                last = [mixed(group * 4 + j, slice(96, 112)) for j in range(4)]
                for b in range(5):
                    value = jnp.zeros((16, 128), F32)
                    for j in range(4):
                        tile = first[j] if b < 4 else last[j]
                        shift = (32 * (j - (b if b < 4 else 0))) % 128
                        moved = tile if shift == 0 else pltpu.roll(tile, shift, 1)
                        value = jnp.where(quarter == j, moved, value)
                    put(b * 16, 16, slice(1024 + group * 128, 1152 + group * 128), value)

    for move in load(step):
        move.wait()
    outs = []
    for q in range(2):
        main = jnp.dot(both_ref[q], high_ref[step, q], preferred_element_type=F32)
        rest = jnp.dot(both_ref[q, 0:80, :], low_ref[step, q], preferred_element_type=F32)
        outs.append(main[0:80] + main[80:160] + rest)
    for half in range(2):
        at = slice(half * 128, (half + 1) * 128)
        even = jnp.where(lane < 64, outs[0][:, at], outs[1][:, at])
        odd = jnp.where(lane < 64, outs[1][:, at], outs[0][:, at])
        base = pl.multiple_of(step * 320 + half * 160, 16)
        sums_ref[pl.ds(base, 80), :] = even
        sums_ref[pl.ds(base + 80, 80), :] = odd

    @pl.when(step == pl.num_programs(0) - 1)
    def _():
        for k in range(13):
            turned = sums_ref[k * 128 : (k + 1) * 128, :].T
            for group in range(8):
                l = 2 * (group % 4) + group // 4
                spread_ref[pl.ds(l * 256 + k, 16, stride=16), :] = turned[group * 16 : (group + 1) * 16]
        for d in range(128):
            out_ref[d] = spread_ref[d * 16 : (d + 1) * 16, :].astype(BF16)


def table_kernel(
    device_ref, codes_ref, logs_ref, coef_ref, colat_ref, rmap_ref, cmap_ref, rsel_ref, csel_ref,
    high_out, low_out, cols_out, rmat_out, state_ref, start_ref, rows_ref,
):
    step = pl.program_id(0)
    first = device_ref[0] * PAIRS

    @pl.when(step == 0)
    def _():
        state_ref[...] = jnp.zeros_like(state_ref)
        log_sine, weight = colat_ref[1], colat_ref[2]
        for i in range(PAIRS):
            for h in range(2):
                order = first + i if h == 0 else M - 1 - first - i
                exponent = logs_ref[order] + order.astype(F32) * log_sine
                ramp = jnp.clip((exponent + 75.0) / 10.0, 0.0, 1.0)
                start_ref[h * PAIRS + i] = jnp.exp(jnp.maximum(exponent, -75.0)) * ramp * weight
        sub = lax.broadcasted_iota(jnp.int32, (128, 256), 0) // 32
        lane = lax.broadcasted_iota(jnp.int32, (128, 256), 1) // 64
        for term in range(20):
            code = codes_ref[0, term % 4, term // 4]
            wide = jnp.dot(rmap_ref[term], rsel_ref[code], preferred_element_type=F32)
            wide = jnp.concatenate([wide] * 4, axis=0)
            rmat_out[term] = jnp.where(sub == lane, wide, 0.0).astype(BF16)
            cols_out[term] = jnp.dot(csel_ref[code], cmap_ref[term], preferred_element_type=F32).astype(BF16)

    cosine = colat_ref[0]

    def advance(base, state, switching):
        state = list(state)
        for k in range(16):
            slot = base + k
            for i in range(PAIRS):
                one, two = state[2 * i], state[2 * i + 1]
                grow = coef_ref[0, (2 * i) * STEPS + slot]
                back = coef_ref[0, (2 * i + 1) * STEPS + slot]
                value = (cosine * grow) * one - two * back
                if switching:
                    value = jnp.where(slot == 0, start_ref[i], value)
                    value = jnp.where(slot == M - first - i, start_ref[PAIRS + i], value)
                state[2 * i], state[2 * i + 1] = value, one
                rows_ref[i, k * 8 : (k + 1) * 8, :] = value
        return tuple(state)

    def sixteen(part, state):
        base = step * CHUNK + part * 16
        switching = (base == 0) | ((base <= M - first) & (base + 16 > M - first - PAIRS))
        state = lax.cond(
            switching, lambda x: advance(base, x, True), lambda x: advance(base, x, False), state
        )
        at = pl.ds(pl.multiple_of(part * 16, 16), 16)
        for i in range(PAIRS):
            for b in range(5):
                value = rows_ref[i, pl.ds(b, 16, stride=8), :]
                high = value.astype(BF16)
                high_out[i, at, b * 128 : (b + 1) * 128] = high
                low_out[i, at, b * 128 : (b + 1) * 128] = (value - high.astype(F32)).astype(BF16)
        return state

    state = lax.fori_loop(0, CHUNK // 16, sixteen, tuple(state_ref[j] for j in range(2 * PAIRS)))
    for j in range(2 * PAIRS):
        state_ref[j] = state[j]


def sums_kernel(first_ref, blocks_ref, high_hbm, low_hbm, out_ref, high_ref, low_ref, sems, spread_ref, turned_ref, left_ref):
    step = pl.program_id(0)

    def load(g):
        return (
            pltpu.make_async_copy(high_hbm.at[g], high_ref.at[g], sems.at[g]),
            pltpu.make_async_copy(low_hbm.at[g], low_ref.at[g], sems.at[PAIRS + g]),
        )

    @pl.when(step == 0)
    def _():
        for g in range(PAIRS):
            for move in load(g):
                move.start()
        lane = lax.broadcasted_iota(jnp.int32, (8, 128), 1)
        for d in range(128):
            spread_ref[d * 16 : (d + 1) * 16, :] = blocks_ref[d].astype(F32)
        for k in range(13):
            parts = [spread_ref[pl.ds(l * 256 + k, 16, stride=16), :] for l in (0, 1, 2, 3, 7, 6, 5, 4)]
            turned_ref[k * 128 : (k + 1) * 128, :] = jnp.concatenate(parts, axis=0).T
        for i in range(PAIRS):
            for h in range(2):
                for b in range(5):
                    north, south = [], []
                    for c in range(2):
                        base = SLOT[(i, h, c)] * 80 + b * 16
                        one, two = turned_ref[base : base + 8, :], turned_ref[base + 8 : base + 16, :]
                        north.append(jnp.where(lane < 64, one, pltpu.roll(two, 64, 1)))
                        south.append(jnp.where(lane < 64, pltpu.roll(one, 64, 1), two))
                    at = slice(b * 128, (b + 1) * 128)
                    left_ref[i, h * 16 : h * 16 + 16, at] = jnp.concatenate(north, axis=0).astype(BF16)
                    left_ref[i, 32 + h * 16 : 48 + h * 16, at] = jnp.concatenate(south, axis=0).astype(BF16)

    for move in load(step):
        move.wait()
    left = left_ref[step]
    both_last = (((1,), (1,)), ((), ()))
    sums = lax.dot_general(left, high_ref[step], both_last, preferred_element_type=F32)
    sums += lax.dot_general(left, low_ref[step], both_last, preferred_element_type=F32)
    pair = first_ref[0] + step
    slot = lax.broadcasted_iota(jnp.int32, (16, STEPS), 1)
    low = sums[0:16] + jnp.where(slot & 1 == 0, sums[32:48], -sums[32:48])
    high = sums[16:32] + jnp.where((slot + pair) & 1 == 0, sums[48:64], -sums[48:64])
    result = jnp.where(slot < M - pair, low, high)
    out_ref[0] = result[:, : M + 1]


def vmem(shape=None, index=None):
    if shape is None:
        return pl.BlockSpec(memory_space=pltpu.VMEM)
    return pl.BlockSpec(shape, index)


SMEM = pl.BlockSpec(memory_space=pltpu.SMEM)
HBM = pl.BlockSpec(memory_space=pltpu.HBM)


def params(limit):
    return pltpu.CompilerParams(vmem_limit_bytes=limit * MIB)


def cost(flops, moved):
    return pl.CostEstimate(flops=flops, bytes_accessed=moved, transcendentals=0)


def recurrence_factors():
    pair = np.arange(M // 2)[:, None]
    slot = np.arange(STEPS)[None, :]
    is_low = slot < M - pair
    order = np.where(is_low, pair, M - 1 - pair)
    degree = np.where(is_low, pair + slot, slot - 1)
    grows = (degree > order) & (slot <= M)
    back = (degree - 1 > order) & (slot <= M)
    n2, l2, m2 = degree.astype(np.float64) ** 2, (degree - 1.0) ** 2, order.astype(np.float64) ** 2
    grow = np.where(grows, np.sqrt(np.where(grows, 4 * n2 - 1, 0) / np.where(grows, n2 - m2, 1)), 0)
    keep = np.where(back, grow * np.sqrt(np.where(back, l2 - m2, 0) / np.where(back, 4 * l2 - 1, 1)), 0)
    return np.stack([grow, keep], axis=1).astype(np.float32).reshape(128, 1, 10 * STEPS)


def selections():
    packed = np.arange(64) % 32 * 2 + np.arange(64) // 32
    rsel, csel = np.zeros((4, 64, 256)), np.zeros((4, 128, 64))
    for code in range(4):
        rows = np.arange(64) if code % 2 else packed
        rows = 63 - rows if code in (1, 2) else rows
        for lev in range(4):
            rsel[code, rows, lev * 64 + np.arange(64)] = 1
        cols = packed if code % 2 else np.arange(64)
        cols = 63 - cols if code in (2, 3) else cols
        csel[code, np.arange(64), cols] = 1
        if code % 2 == 0:
            csel[code, 64 + np.arange(64), cols] = 1
    return rsel.astype(BF16), csel.astype(BF16)


def legendre_table(device, codes, row_map, col_map):
    terms = 0.5 * np.log1p(0.5 / np.arange(1, M, dtype=np.float64))
    logs = (np.concatenate([np.zeros(1), np.cumsum(terms)]) + 0.5 * math.log(0.5)).astype(np.float32)
    colat = latitudes()
    weight = np.pi * np.sin(colat) * math.sqrt(NLAT) / (NLAT + 0.5)
    colat = np.stack([np.cos(colat), np.log(np.sin(colat)), weight]).astype(np.float32)
    rsel, csel = selections()
    shape = (PAIRS, STEPS, 640)
    block = vmem((PAIRS, CHUNK, 640), lambda g, d: (0, g, 0))
    cols = (20, 128, 160)
    rmat = (20, 128, 256)
    whole = lambda g, d: (0, 0, 0)
    own = pl.BlockSpec((None, 1, 10 * STEPS), lambda g, d: (d[0], 0, 0), memory_space=pltpu.SMEM)
    return pl.pallas_call(
        table_kernel,
        out_shape=tuple(jax.ShapeDtypeStruct(made, BF16) for made in (shape, shape, cols, rmat)),
        grid_spec=pltpu.PrefetchScalarGridSpec(
            num_scalar_prefetch=1,
            grid=(STEPS // CHUNK,),
            in_specs=[SMEM, SMEM, own] + [vmem()] * 5,
            out_specs=(block, block, vmem(cols, whole), vmem(rmat, whole)),
            scratch_shapes=[
                pltpu.VMEM((2 * PAIRS, 8, 128), F32),
                pltpu.VMEM((2 * PAIRS, 8, 128), F32),
                pltpu.VMEM((PAIRS, 128, 128), F32),
            ],
        ),
        compiler_params=params(57),
        cost_estimate=cost(60_000_000, 60_000_000),
        name="legendre_table",
    )(
        device, codes, jnp.asarray(logs), jnp.asarray(recurrence_factors()), jnp.asarray(colat), row_map, col_map,
        jnp.asarray(rsel), jnp.asarray(csel),
    )


def body(source, row_map, col_map, pattern, codes, need_list, owner):
    lat_me = lax.axis_index("lat").astype(jnp.int32)
    tile_me = lax.axis_index("tile").astype(jnp.int32)
    device = tile_me * lax.axis_size("lat") + lat_me
    first = device * PAIRS
    me = lat_me.reshape(1)
    needs = need_list[0]
    outgoing = pl.pallas_call(
        pack_kernel,
        out_shape=jax.ShapeDtypeStruct((8 * MOST, 64, 512), BF16),
        in_specs=[SMEM, SMEM, SMEM, HBM],
        out_specs=vmem(),
        scratch_shapes=[
            pltpu.VMEM((7, 8, 4096), BF16),
            pltpu.VMEM((2, 256, 128), F32),
            pltpu.VMEM((7, 64, 512), BF16),
            pltpu.SMEM((8 * MOST + 1,), jnp.int32),
            pltpu.SemaphoreType.DMA((7,)),
        ],
        compiler_params=params(57),
        cost_estimate=cost(1_000_000, 2_000_000),
        name="pack",
    )(owner, needs, me, source)
    incoming = lax.all_to_all(outgoing, "lat", split_axis=0, concat_axis=0, tiled=True)

    code = jnp.transpose(codes, (1, 2, 0))
    table_high, table_low = (jnp.asarray(t) for t in dft_tables())
    high, low, cols, rmat = legendre_table(
        device.reshape(1), code, row_map.reshape(20, 32, 64), col_map.reshape(20, 64, 160)
    )

    field = pl.pallas_call(
        regrid_kernel,
        out_shape=jax.ShapeDtypeStruct((16, 112, 128), BF16),
        in_specs=[SMEM] * 5 + [HBM] * 3,
        out_specs=vmem(),
        scratch_shapes=[
            pltpu.VMEM((NEED, 64, 512), BF16),
            pltpu.VMEM((20, 128, 160), BF16),
            pltpu.VMEM((20, 128, 256), BF16),
            pltpu.SemaphoreType.DMA((NEED + 2,)),
            pltpu.VMEM((2 * NEED, 512, 128), BF16),
            pltpu.VMEM((2, 256, 128), F32),
            pltpu.VMEM((2, 256, 128), F32),
            pltpu.VMEM((16, 16, 128), F32),
            pltpu.SMEM((8,), jnp.int32),
        ],
        compiler_params=params(57),
        cost_estimate=cost(700_000_000, 5_000_000),
        name="regrid",
    )(owner, needs, me, jnp.transpose(pattern, (1, 2, 0)), code, incoming, cols, rmat)
    rows = lax.all_to_all(field, "tile", split_axis=0, concat_axis=0, tiled=True)

    spectral = pl.pallas_call(
        dft_kernel,
        grid=(5,),
        out_shape=jax.ShapeDtypeStruct((128, 16, 128), BF16),
        in_specs=[vmem(), HBM, HBM],
        out_specs=vmem((128, 16, 128), lambda g: (0, 0, 0)),
        scratch_shapes=[
            pltpu.VMEM((5, 2, 1280, 256), BF16),
            pltpu.VMEM((5, 2, 1280, 256), BF16),
            pltpu.SemaphoreType.DMA((10,)),
            pltpu.VMEM((2, 160, 1280), BF16),
            pltpu.VMEM((1664, 128), F32),
            pltpu.VMEM((2048, 128), F32),
        ],
        compiler_params=params(57),
        cost_estimate=cost(1_000_000_000, 14_000_000),
        name="dft",
    )(rows, table_high, table_low)
    arranged = lax.all_to_all(spectral, ("lat", "tile"), split_axis=0, concat_axis=0, tiled=True)

    return pl.pallas_call(
        sums_kernel,
        grid=(PAIRS,),
        out_shape=jax.ShapeDtypeStruct((PAIRS, 2 * LEV, M + 1), F32),
        in_specs=[SMEM, vmem(), HBM, HBM],
        out_specs=vmem((1, 2 * LEV, M + 1), lambda g: (g, 0, 0)),
        scratch_shapes=[
            pltpu.VMEM((PAIRS, STEPS, 640), BF16),
            pltpu.VMEM((PAIRS, STEPS, 640), BF16),
            pltpu.SemaphoreType.DMA((2 * PAIRS,)),
            pltpu.VMEM((2048, 128), F32),
            pltpu.VMEM((1664, 128), F32),
            pltpu.VMEM((PAIRS, 64, 640), BF16),
        ],
        compiler_params=params(57),
        cost_estimate=cost(2_000_000_000, 17_000_000),
        name="sums",
    )(first.reshape(1), arranged, high, low)


def solution(mesh):
    placed = (
        P(("tile", "lat"), None, None),
        P("lat", "tile", None, None, None),
        P("lat", None, None, "tile"),
        P("lat", "tile", None),
        P("lat", "tile", None),
        P("tile", None, None),
        P(),
    )
    return jax.shard_map(
        body, mesh=mesh, in_specs=placed, out_specs=P(("tile", "lat"), None, None), check_vma=False
    )
```

time: 127 us -> 96.2 us (0.76)
  local copies, waits for them, and re-layouts: 42.4 us -> 1.97 us
  blocking collectives: 0 us -> 15.5 us
  starting transfers between devices: 21.3 us -> 13.5 us
  other arithmetic: 7.17 us -> 0 us
  waiting for transfers between devices: 9.09 us -> 16.1 us
  Pallas kernels: 45.7 us -> 48.5 us
    unnamed x59 -> x4, local copies, waits for them, and re-layouts: 23.4 us -> 1.97 us
    all_to_all x0 -> x1, blocking collectives: none -> 15.5 us  [body(): lax.all_to_all(field, 'tile', split_axis=0, concat_axis=0, tiled=True)]
    all_to_all x1, waiting for transfers between devices: 0.01 us -> 13.4 us  [body(): lax.all_to_all(spectral, ('lat', 'tile'), split_axis=0, concat_axis=0, ti...]
    mul x4 -> x0, local copies, waits for them, and re-layouts: 9.32 us -> none  [body(): eye[None, :, None, :, None] * rmap[:, None, :, None, :]]
    all_to_all x1 -> x0, waiting for transfers between devices: 9.08 us -> none  [body(): lax.all_to_all(field, 'tile', split_axis=0, concat_axis=0, tiled=True)]
    all_to_all x1 -> x0, starting transfers between devices: 6.55 us -> none  [body(): lax.all_to_all(field, 'tile', split_axis=0, concat_axis=0, tiled=True)]
    rev x4 -> x0, local copies, waits for them, and re-layouts: 4.02 us -> none  [the longest x1 1.88 us: body(): cmap[:, ::-1, :]]
    reshape x7 -> x0, local copies, waits for them, and re-layouts: 3.46 us -> none  [the longest x2 2.37 us: body(): cmap.reshape(20, 32, 2, 160)]
  transfers between devices with their start and end apart: 3 -> 2, of which waited for: 1 -> 2; matrix products, arithmetic and copies ran while one was open for 20% -> 0% of each run, Pallas kernels for 15% -> 19%
where the time goes in v2:
time: 96.2 us; the launch traced here: 95.6 us
  Pallas kernels  48.5 us (50%)
  waiting for transfers between devices  16.1 us (17%)
  blocking collectives  15.5 us (16%)
  starting transfers between devices  13.5 us (14%)
  local copies, waits for them, and re-layouts  1.97 us (2%)
    pallas_call x1, Pallas kernels, legendre_table(): pl.pallas_call(table_kernel, out_shape=tuple((jax.ShapeDtypeStruct(made,...  18 us
    all_to_all x1, blocking collectives, body(): lax.all_to_all(field, 'tile', split_axis=0, concat_axis=0, tiled=True)  15.5 us
    all_to_all x1, waiting for transfers between devices, body(): lax.all_to_all(spectral, ('lat', 'tile'), split_axis=0, concat_axis=0, ti...  13.4 us
    pallas_call x1, Pallas kernels, body(): pl.pallas_call(regrid_kernel, out_shape=jax.ShapeDtypeStruct((16, 112, 12...  9.51 us
    pallas_call x1, Pallas kernels, body(): pl.pallas_call(sums_kernel, grid=(PAIRS,), out_shape=jax.ShapeDtypeStruct...  9.28 us
    pallas_call x1, Pallas kernels, body(): pl.pallas_call(dft_kernel, grid=(5,), out_shape=jax.ShapeDtypeStruct((128...  7.67 us
    all_to_all x1, starting transfers between devices, body(): lax.all_to_all(outgoing, 'lat', split_axis=0, concat_axis=0, tiled=True)  6.83 us
    all_to_all x1, starting transfers between devices, body(): lax.all_to_all(spectral, ('lat', 'tile'), split_axis=0, concat_axis=0, ti...  6.68 us
  transfers between devices with their start and end apart: 2, of which 2 were waited for; matrix products, arithmetic and copies ran while one was open for 0% of the time, Pallas kernels for 19%

profile of v2, /device:TPU:1, one launch (start us, length us, event | category | flops | bytes accessed | tf_op | source)
XLA Modules:
  0.0 95.6 jit_solution(6136964669029920184)
XLA Ops:
  0.0 4.1 %pack.1 = bf16[24,64,512]{2,1,0:T(8,128)(2,1)} custom-call(s32[896]{0:T(1024)} %owner_ref.3, s32[8,12]{1,0:T(8,128)} %bitcast.10, s32[1]{0:T(128)} %bitcast.2.me_ref, bf16[7,8,4096]{2,1,0:T(8,128)(2,1)} %source_hbm.1), custom_call_target="tpu_custom_call" | custom-call | flops 1000000 | bytes 2000000 | tf_op jit(solution)/shard_map/pack/pallas_call | solution.py:434
  4.1 6.8 %all-to-all-start = ((bf16[24,64,512]{2,1,0:T(8,128)(2,1)}), bf16[24,64,512]{2,1,0:T(8,128)(2,1)S(1)}, u32[]{:S(2)}, u32[]{:S(2)}) async-start(bf16[24,64,512]{2,1,0:T(8,128)(2,1)} %pack.1), calls=%async_computation | async-start | bytes 3145728 | tf_op jit(solution)/shard_map/all_to_all | solution.py:450
  10.9 18.0 %legendre_table.1 = (bf16[5,1296,640]{2,1,0:T(8,128)(2,1)}, bf16[5,1296,640]{2,1,0:T(8,128)(2,1)}, bf16[20,128,160]{2,1,0:T(8,128)(2,1)}, bf16[20,128,256]{2,1,0:T(8,128)(2,1)}) custom-call(s32[1]{0:T(128)} %bitcast.5.device_ref, s32[1,4,5]{2,1,0:T(4,128)} %bitcast.12, f32[1280]{0:T(1024)} %constant.29.clone.logs_ref, ...), custom_call_target="tpu_custom_call" | custom-call | flops 60000000 | bytes 60000000 | tf_op jit(solution)/shard_map/legendre_table/pallas_call | solution.py:404
  28.9 2.8 %all-to-all-done.blocks_hbm = bf16[24,64,512]{2,1,0:T(8,128)(2,1)S(1)} async-done(((bf16[24,64,512]{2,1,0:T(8,128)(2,1)}), bf16[24,64,512]{2,1,0:T(8,128)(2,1)S(1)}, u32[]{:S(2)}, u32[]{:S(2)}) %all-to-all-start) | async-done | bytes 1572896 | tf_op jit(solution)/shard_map/all_to_all | solution.py:450
  31.6 0.0 copy-start
  31.6 1.2 %copy-done = bf16[24,64,512]{2,1,0:T(8,128)(2,1)} copy-done((bf16[24,64,512]{2,1,0:T(8,128)(2,1)}, bf16[24,64,512]{2,1,0:T(8,128)(2,1)S(1)}, u32[]{:S(2)}) %copy-start) | copy-done | bytes 1572888
  32.8 9.5 %regrid.1 = bf16[16,112,128]{2,1,0:T(8,128)(2,1)} custom-call(s32[896]{0:T(1024)} %owner_ref.3, s32[8,12]{1,0:T(8,128)} %bitcast.11, s32[1]{0:T(128)} %bitcast.2.me_ref, s32[1,4,5]{2,1,0:T(4,128)} %bitcast.14, s32[1,4,5]{2,1,0:T(4,128)} %bitcast.13, bf16[24,64,512]{2,1,0:T(8,128)(2,1)} %copy-done, bf16[20,128,160]{2,1,0:T(8,128)(2,1)} %get-tuple-element.9.cols_hbm, ...), custom_call_target="tpu_custom_call" | custom-call | flops 700000000 | bytes 5000000 | tf_op jit(solution)/shard_map/regrid/pallas_call | solution.py:458
  42.3 15.5 %all_to_all.15.rows_ref = bf16[16,112,128]{2,1,0:T(8,128)(2,1)} all-to-all(bf16[16,112,128]{2,1,0:T(8,128)(2,1)} %regrid.1), channel_id=1, replica_groups=mesh['tile'=16,'lat'=8] {'tile'}, dimensions={0} | all-to-all | bytes 917504 | tf_op jit(solution)/shard_map/all_to_all | solution.py:478
  57.8 7.7 %dft.1 = bf16[128,16,128]{2,1,0:T(8,128)(2,1)} custom-call(bf16[16,112,128]{2,1,0:T(8,128)(2,1)} %all_to_all.15.rows_ref, bf16[5,2,1280,256]{3,2,1,0:T(8,128)(2,1)} %constant.27.clone.high_hbm, bf16[5,2,1280,256]{3,2,1,0:T(8,128)(2,1)} %constant.28.clone.low_hbm), custom_call_target="tpu_custom_call" | custom-call | flops 1000000000 | bytes 14000000 | tf_op jit(solution)/shard_map/dft/pallas_call | solution.py:480
  65.5 6.7 %all-to-all-start.2 = ((bf16[128,16,128]{2,1,0:T(8,128)(2,1)}), bf16[128,16,128]{2,1,0:T(8,128)(2,1)S(1)}, u32[]{:S(2)}, u32[]{:S(2)}) async-start(bf16[128,16,128]{2,1,0:T(8,128)(2,1)} %dft.1), calls=%async_computation.2 | async-start | bytes 1048576 | tf_op jit(solution)/shard_map/all_to_all | solution.py:498
  72.2 13.4 %all-to-all-done.2.blocks_ref = bf16[128,16,128]{2,1,0:T(8,128)(2,1)S(1)} async-done(((bf16[128,16,128]{2,1,0:T(8,128)(2,1)}), bf16[128,16,128]{2,1,0:T(8,128)(2,1)S(1)}, u32[]{:S(2)}, u32[]{:S(2)}) %all-to-all-start.2) | async-done | bytes 524320 | tf_op jit(solution)/shard_map/all_to_all | solution.py:498
  85.5 0.0 copy-start.1
  85.5 0.8 copy-done.1
  86.3 9.3 %sums.1 = f32[5,16,1281]{2,1,0:T(8,128)} custom-call(s32[1]{0:T(128)} %bitcast.first_ref, bf16[128,16,128]{2,1,0:T(8,128)(2,1)} %copy-done.1, bf16[5,1296,640]{2,1,0:T(8,128)(2,1)} %get-tuple-element.11.high_hbm, bf16[5,1296,640]{2,1,0:T(8,128)(2,1)} %get-tuple-element.12.low_hbm), custom_call_target="tpu_custom_call" | custom-call | flops 2000000000 | bytes 17000000 | tf_op jit(solution)/shard_map/sums/pallas_call | solution.py:500
Async XLA Ops:
  4.1 27.5 %all-to-all-start = ((bf16[24,64,512]{2,1,0:T(8,128)(2,1)}), bf16[24,64,512]{2,1,0:T(8,128)(2,1)S(1)}, u32[]{:S(2)}, u32[]{:S(2)}) async-start(bf16[24,64,512]{2,1,0:T(8,128)(2,1)} %pack.1), calls=%async_computation | async-start | bytes 3145728 | tf_op jit(solution)/shard_map/all_to_all | solution.py:450
  31.6 1.2 %copy-start = (bf16[24,64,512]{2,1,0:T(8,128)(2,1)}, bf16[24,64,512]{2,1,0:T(8,128)(2,1)S(1)}, u32[]{:S(2)}) copy-start(bf16[24,64,512]{2,1,0:T(8,128)(2,1)S(1)} %all-to-all-done.blocks_hbm) | copy-start | bytes 4718596
  65.5 20.0 %all-to-all-start.2 = ((bf16[128,16,128]{2,1,0:T(8,128)(2,1)}), bf16[128,16,128]{2,1,0:T(8,128)(2,1)S(1)}, u32[]{:S(2)}, u32[]{:S(2)}) async-start(bf16[128,16,128]{2,1,0:T(8,128)(2,1)} %dft.1), calls=%async_computation.2 | async-start | bytes 1048576 | tf_op jit(solution)/shard_map/all_to_all | solution.py:498
  85.5 0.8 copy-start.1

commit v3 on v2

v3 whole, which is shorter than its diff:
```python
import math

import jax
import jax.numpy as jnp
import numpy as np
from jax import lax
from jax.experimental import pallas as pl
from jax.experimental.pallas import tpu as pltpu
from jax.sharding import PartitionSpec as P

NLON = 2560
NLAT = 1280
M = 1280
NEED = 12
MOST = 3
LEV = 8
PAIRS = 5
STEPS = 1296
CHUNK = 144
MIB = 2**20
F32 = jnp.float32
BF16 = jnp.bfloat16

EVENS = [(i, h, c) for i in range(5) for h in range(2) if (i + h) % 2 == 0 for c in range(2)]
ODDS = [(i, h, c) for i in range(5) for h in range(2) if (i + h) % 2 == 1 for c in range(2)]
SLOT = {e: 2 * w for w, e in enumerate(EVENS)} | {e: 2 * w + 1 for w, e in enumerate(ODDS)}


def dft_tables():
    s = np.arange(8)
    points = np.concatenate(
        [(s[:, None] * 160 + np.arange(128)).ravel(), (s[:, None] * 160 + np.arange(128, 160)).ravel()]
    )
    l2, t = np.meshgrid(np.arange(4), np.arange(16), indexing="ij")
    order = np.zeros((2, 10, 2, 64), np.int64)
    part = np.zeros((2, 10, 2, 64), np.int64)
    for q in range(2):
        for w in range(10):
            for half in range(2):
                i, h, c = (EVENS if q == half else ODDS)[w]
                pair = 5 * (t * 8 + 2 * l2 + half) + i
                order[q, w, half] = (pair if h == 0 else M - 1 - pair).ravel()
                part[q, w, half] = c
    order, part = order.reshape(2, 1, 1280), part.reshape(2, 1, 1280)
    angle = (points[None, :, None] * order % NLON) * (2.0 * np.pi / NLON)
    table = np.where(part == 0, np.cos(angle), -np.sin(angle)) / math.sqrt(NLON)
    high = table.astype(BF16)
    low = (table - high.astype(np.float64)).astype(BF16)
    both = np.stack([x.reshape(2, 1280, 5, 256).transpose(2, 0, 1, 3) for x in (high, low)], axis=1)
    return np.ascontiguousarray(both)


def latitudes():
    b, a2, l, t = np.meshgrid(np.arange(5), np.arange(2), np.arange(4), np.arange(16), indexing="ij")
    lat = (l * 160 + b * 32 + 2 * t + a2).reshape(5, 128)
    colat = np.pi * (lat + 0.75) / (NLAT + 0.5)
    return np.concatenate([colat, np.full((3, 128), np.pi / 2)])


def holder_of(owner_ref, need_ref, dest, i):
    holder = owner_ref[need_ref[dest, i]]
    device = (holder * 9363) >> 16
    return device & 7, holder - 7 * device


def pack_kernel(owner_ref, need_ref, me_ref, source_hbm, out_hbm, source_ref, rows_ref, turned_ref, list_ref, sems):
    loads = [pltpu.make_async_copy(source_hbm.at[s], source_ref.at[s], sems.at[s]) for s in range(7)]
    for load in loads:
        load.start()
    lane = lax.broadcasted_iota(jnp.int32, (32, 128), 1)
    me = me_ref[0]
    for at in range(8 * MOST):
        list_ref[at] = 0
    for dest in range(8):
        count = jnp.int32(0)
        for i in range(NEED):
            lat, slot = holder_of(owner_ref, need_ref, dest, i)
            hit = lat == me
            list_ref[jnp.where(hit, dest * MOST + jnp.minimum(count, MOST - 1), 8 * MOST)] = slot
            count = count + hit.astype(jnp.int32)
    for s in range(7):
        loads[s].wait()
        for i in range(32):
            rows_ref[s % 2, pl.ds(i, 8, stride=32), :] = source_ref[s, :, i * 128 : (i + 1) * 128].astype(F32)
        for lp in range(4):
            one = rows_ref[s % 2, lp * 64 : lp * 64 + 32, :]
            two = rows_ref[s % 2, lp * 64 + 32 : lp * 64 + 64, :]
            top = jnp.where(lane < 64, one, pltpu.roll(two, 64, 1))
            low = jnp.where(lane < 64, pltpu.roll(one, 64, 1), two)
            at = slice(lp * 128, (lp + 1) * 128)
            turned_ref[s, 0:32, at] = top.astype(BF16)
            turned_ref[s, 32:64, at] = low.astype(BF16)
    stores = [
        pltpu.make_async_copy(turned_ref.at[list_ref[at]], out_hbm.at[at], sems.at[7 + at]) for at in range(8 * MOST)
    ]
    for store in stores:
        store.start()
    for store in stores:
        store.wait()


def regrid_kernel(
    owner_ref, need_ref, me_ref, pattern_ref, codes_ref, blocks_ref, maps_hbm, out_ref,
    maps_ref, sems, forms_ref, acc_ref, tail_ref, packed_ref, seen_ref,
):
    me = me_ref[0]
    south = me >= 4
    row_blocks = [jnp.where(south, 4 - b, b) for b in range(5)]
    loads = [
        pltpu.make_async_copy(maps_hbm.at[pl.ds(row_blocks[b] * 4, 4)], maps_ref.at[b * 4 : b * 4 + 4], sems.at[b])
        for b in range(5)
    ]
    for load in loads:
        load.start()
    for l in range(8):
        seen_ref[l] = 0
    tail_ref[...] = jnp.zeros_like(tail_ref)
    lane = lax.broadcasted_iota(jnp.int32, (64, 128), 1)
    zero = jnp.zeros((64, 128), BF16)
    places = []
    for i in range(NEED):
        lat, _ = holder_of(owner_ref, need_ref, me, i)
        rank = seen_ref[lat]
        at = lat * MOST + jnp.minimum(rank, MOST - 1)
        seen_ref[lat] = rank + 1
        places.append(at)
    for i in range(NEED):
        for lp in range(0, 4, 2):
            tiles = [blocks_ref[places[i], :, (lp + j) * 128 : (lp + j + 1) * 128] for j in range(2)]
            both = jnp.concatenate(tiles, axis=0).astype(F32).T.astype(BF16)
            for j, tile in enumerate(tiles):
                at = (lp + j) * 128
                forms_ref[2 * i, at : at + 64, :] = jnp.where(lane < 64, tile, zero)
                forms_ref[2 * i, at + 64 : at + 128, :] = jnp.where(lane < 64, zero, tile)
                for half in range(2):
                    part = both[half * 64 : half * 64 + 64]
                    picked = jnp.where(lane < 64, part, zero) if j == 0 else jnp.where(lane < 64, zero, part)
                    forms_ref[2 * i + 1, at + half * 64 : at + half * 64 + 64, :] = picked

    for b in range(5):
        loads[b].wait()
        sums = [None, None]
        for k in range(4):
            term = b * 4 + k
            form = forms_ref[pattern_ref[0, k, row_blocks[b]] * 2 + (codes_ref[0, k, row_blocks[b]] & 1)]
            inner = jnp.dot(form, maps_ref[term, :, 0:160], preferred_element_type=F32).astype(BF16)
            for half in range(2):
                new = jnp.dot(
                    maps_ref[term, :, 256:512], inner[half * 256 : (half + 1) * 256], preferred_element_type=F32
                )
                sums[half] = new if k == 0 else sums[half] + new
        for half in range(2):
            acc_ref[b % 2, half * 128 : (half + 1) * 128, :] = sums[half][:, :128]
            tail_ref[b % 2, half * 128 : (half + 1) * 128, 0:32] = sums[half][:, 128:160]
        for t in range(16):
            at = [jnp.where(south, 31 - (2 * t + a), 2 * t + a) for a in range(2)]
            main = [acc_ref[b % 2, pl.ds(at[a], 8, stride=32), :] for a in range(2)]
            out_ref[t, b * 16 : (b + 1) * 16, :] = jnp.concatenate(main, axis=0).astype(BF16)
            rest = jnp.concatenate([tail_ref[b % 2, pl.ds(at[a], 8, stride=32), :] for a in range(2)], axis=0)
            if b == 0:
                packed_ref[t] = rest
            elif b < 4:
                packed_ref[t] += pltpu.roll(rest, 32 * b, 1)
            else:
                out_ref[t, 96:112, :] = rest.astype(BF16)
    for t in range(16):
        out_ref[t, 80:96, :] = packed_ref[t].astype(BF16)


def dft_kernel(rows_ref, table_hbm, out_ref, table_ref, sems, both_ref, sums_ref, spread_ref):
    lane = lax.broadcasted_iota(jnp.int32, (80, 128), 1)
    loads = [pltpu.make_async_copy(table_hbm.at[g], table_ref.at[g], sems.at[g]) for g in range(5)]
    for load in loads:
        load.start()
    quarter = lax.broadcasted_iota(jnp.int32, (16, 128), 1) // 32
    sums_ref[1600:1664, :] = jnp.zeros((64, 128), F32)
    for q in range(2):

        def mixed(s, at):
            one, two = rows_ref[s, at, :].astype(F32), rows_ref[s + 8, at, :].astype(F32)
            return one + two if q == 0 else one - two

        def put(row, count, at, value):
            high = value.astype(BF16)
            both_ref[q, row : row + count, at] = high
            both_ref[q, 80 + row : 80 + row + count, at] = (value - high.astype(F32)).astype(BF16)

        for s in range(8):
            put(0, 80, slice(s * 128, (s + 1) * 128), mixed(s, slice(0, 80)))
        for group in range(2):
            first = [mixed(group * 4 + j, slice(80, 96)) for j in range(4)]
            last = [mixed(group * 4 + j, slice(96, 112)) for j in range(4)]
            for b in range(5):
                value = jnp.zeros((16, 128), F32)
                for j in range(4):
                    tile = first[j] if b < 4 else last[j]
                    shift = (32 * (j - (b if b < 4 else 0))) % 128
                    moved = tile if shift == 0 else pltpu.roll(tile, shift, 1)
                    value = jnp.where(quarter == j, moved, value)
                put(b * 16, 16, slice(1024 + group * 128, 1152 + group * 128), value)

    for step in range(5):
        loads[step].wait()
        outs = []
        for q in range(2):
            main = jnp.dot(both_ref[q], table_ref[step, 0, q], preferred_element_type=F32)
            rest = jnp.dot(both_ref[q, 0:80, :], table_ref[step, 1, q], preferred_element_type=F32)
            outs.append(main[0:80] + main[80:160] + rest)
        for half in range(2):
            at = slice(half * 128, (half + 1) * 128)
            even = jnp.where(lane < 64, outs[0][:, at], outs[1][:, at])
            odd = jnp.where(lane < 64, outs[1][:, at], outs[0][:, at])
            base = step * 320 + half * 160
            sums_ref[base : base + 80, :] = even
            sums_ref[base + 80 : base + 160, :] = odd
    for k in range(13):
        turned = sums_ref[k * 128 : (k + 1) * 128, :].T
        for group in range(8):
            l = 2 * (group % 4) + group // 4
            spread_ref[pl.ds(l * 256 + k, 16, stride=16), :] = turned[group * 16 : (group + 1) * 16]
    for d in range(128):
        out_ref[d] = spread_ref[d * 16 : (d + 1) * 16, :].astype(BF16)


def table_kernel(
    device_ref, codes_ref, logs_ref, coef_ref, colat_ref, rmap_ref, cmap_ref, rsel_ref, csel_ref,
    legendre_out, maps_out, state_ref, start_ref, rows_ref,
):
    step = pl.program_id(0)
    first = device_ref[0] * PAIRS

    @pl.when(step == 0)
    def _():
        state_ref[...] = jnp.zeros_like(state_ref)
        log_sine, weight = colat_ref[1], colat_ref[2]
        for i in range(PAIRS):
            for h in range(2):
                order = first + i if h == 0 else M - 1 - first - i
                exponent = logs_ref[order] + order.astype(F32) * log_sine
                ramp = jnp.clip((exponent + 75.0) / 10.0, 0.0, 1.0)
                start_ref[h * PAIRS + i] = jnp.exp(jnp.maximum(exponent, -75.0)) * ramp * weight
        sub = lax.broadcasted_iota(jnp.int32, (128, 256), 0) // 32
        lane = lax.broadcasted_iota(jnp.int32, (128, 256), 1) // 64
        for term in range(20):
            code = codes_ref[0, term % 4, term // 4]
            wide = jnp.dot(rmap_ref[term], rsel_ref[code], preferred_element_type=F32)
            wide = jnp.concatenate([wide] * 4, axis=0)
            maps_out[term, :, 256:512] = jnp.where(sub == lane, wide, 0.0).astype(BF16)
            maps_out[term, :, 0:160] = jnp.dot(csel_ref[code], cmap_ref[term], preferred_element_type=F32).astype(BF16)

    cosine = colat_ref[0]

    def advance(base, state, switching):
        state = list(state)
        for k in range(16):
            slot = base + k
            for i in range(PAIRS):
                one, two = state[2 * i], state[2 * i + 1]
                grow = coef_ref[0, (2 * i) * STEPS + slot]
                back = coef_ref[0, (2 * i + 1) * STEPS + slot]
                value = (cosine * grow) * one - two * back
                if switching:
                    value = jnp.where(slot == 0, start_ref[i], value)
                    value = jnp.where(slot == M - first - i, start_ref[PAIRS + i], value)
                state[2 * i], state[2 * i + 1] = value, one
                rows_ref[i, k * 8 : (k + 1) * 8, :] = value
        return tuple(state)

    def sixteen(part, state):
        base = step * CHUNK + part * 16
        switching = (base == 0) | ((base <= M - first) & (base + 16 > M - first - PAIRS))
        state = lax.cond(
            switching, lambda x: advance(base, x, True), lambda x: advance(base, x, False), state
        )
        at = pl.ds(pl.multiple_of(part * 16, 16), 16)
        for i in range(PAIRS):
            for b in range(5):
                value = rows_ref[i, pl.ds(b, 16, stride=8), :]
                high = value.astype(BF16)
                legendre_out[i, at, b * 128 : (b + 1) * 128] = high
                legendre_out[i, at, 640 + b * 128 : 768 + b * 128] = (value - high.astype(F32)).astype(BF16)
        return state

    state = lax.fori_loop(0, CHUNK // 16, sixteen, tuple(state_ref[j] for j in range(2 * PAIRS)))
    for j in range(2 * PAIRS):
        state_ref[j] = state[j]


def sums_kernel(
    first_ref, blocks_ref, table_hbm, out_hbm, table_ref, out_ref, sems, spread_ref, turned_ref, left_ref,
):
    loads = [pltpu.make_async_copy(table_hbm.at[i], table_ref.at[i], sems.at[i]) for i in range(PAIRS)]
    stores = [pltpu.make_async_copy(out_ref.at[i], out_hbm.at[i], sems.at[PAIRS + i]) for i in range(PAIRS)]
    for load in loads:
        load.start()
    lane = lax.broadcasted_iota(jnp.int32, (8, 128), 1)
    for d in range(128):
        spread_ref[d * 16 : (d + 1) * 16, :] = blocks_ref[d].astype(F32)
    for k in range(13):
        parts = [spread_ref[pl.ds(l * 256 + k, 16, stride=16), :] for l in (0, 1, 2, 3, 7, 6, 5, 4)]
        turned_ref[k * 128 : (k + 1) * 128, :] = jnp.concatenate(parts, axis=0).T
    for i in range(PAIRS):
        for h in range(2):
            for b in range(5):
                north, south = [], []
                for c in range(2):
                    base = SLOT[(i, h, c)] * 80 + b * 16
                    one, two = turned_ref[base : base + 8, :], turned_ref[base + 8 : base + 16, :]
                    north.append(jnp.where(lane < 64, one, pltpu.roll(two, 64, 1)))
                    south.append(jnp.where(lane < 64, pltpu.roll(one, 64, 1), two))
                at, again = slice(b * 128, (b + 1) * 128), slice(640 + b * 128, 768 + b * 128)
                north = jnp.concatenate(north, axis=0).astype(BF16)
                left_ref[i, h * 16 : h * 16 + 16, at] = north
                left_ref[i, h * 16 : h * 16 + 16, again] = north
                south = jnp.concatenate(south, axis=0).astype(BF16)
                left_ref[i, 32 + h * 16 : 48 + h * 16, at] = south
                left_ref[i, 32 + h * 16 : 48 + h * 16, again] = south

    slot = lax.broadcasted_iota(jnp.int32, (16, STEPS), 1)
    for i in range(PAIRS):
        loads[i].wait()
        sums = lax.dot_general(left_ref[i], table_ref[i], (((1,), (1,)), ((), ())), preferred_element_type=F32)
        pair = first_ref[0] + i
        low = sums[0:16] + jnp.where(slot & 1 == 0, sums[32:48], -sums[32:48])
        high = sums[16:32] + jnp.where((slot + pair) & 1 == 0, sums[48:64], -sums[48:64])
        result = jnp.where(slot < M - pair, low, high)
        out_ref[i] = result[:, : M + 1]
        stores[i].start()
    for store in stores:
        store.wait()


def vmem(shape=None, index=None):
    if shape is None:
        return pl.BlockSpec(memory_space=pltpu.VMEM)
    return pl.BlockSpec(shape, index)


SMEM = pl.BlockSpec(memory_space=pltpu.SMEM)
HBM = pl.BlockSpec(memory_space=pltpu.HBM)


def params(limit):
    return pltpu.CompilerParams(vmem_limit_bytes=limit * MIB)


def cost(flops, moved):
    return pl.CostEstimate(flops=flops, bytes_accessed=moved, transcendentals=0)


def recurrence_factors():
    pair = np.arange(M // 2)[:, None]
    slot = np.arange(STEPS)[None, :]
    is_low = slot < M - pair
    order = np.where(is_low, pair, M - 1 - pair)
    degree = np.where(is_low, pair + slot, slot - 1)
    grows = (degree > order) & (slot <= M)
    back = (degree - 1 > order) & (slot <= M)
    n2, l2, m2 = degree.astype(np.float64) ** 2, (degree - 1.0) ** 2, order.astype(np.float64) ** 2
    grow = np.where(grows, np.sqrt(np.where(grows, 4 * n2 - 1, 0) / np.where(grows, n2 - m2, 1)), 0)
    keep = np.where(back, grow * np.sqrt(np.where(back, l2 - m2, 0) / np.where(back, 4 * l2 - 1, 1)), 0)
    return np.stack([grow, keep], axis=1).astype(np.float32).reshape(128, 1, 10 * STEPS)


def selections():
    packed = np.arange(64) % 32 * 2 + np.arange(64) // 32
    rsel, csel = np.zeros((4, 64, 256)), np.zeros((4, 128, 64))
    for code in range(4):
        rows = np.arange(64) if code % 2 else packed
        rows = 63 - rows if code in (1, 2) else rows
        for lev in range(4):
            rsel[code, rows, lev * 64 + np.arange(64)] = 1
        cols = packed if code % 2 else np.arange(64)
        cols = 63 - cols if code in (2, 3) else cols
        csel[code, np.arange(64), cols] = 1
        csel[code, 64 + np.arange(64), cols] = 1
    return rsel.astype(BF16), csel.astype(BF16)


def legendre_table(device, codes, row_map, col_map):
    terms = 0.5 * np.log1p(0.5 / np.arange(1, M, dtype=np.float64))
    logs = (np.concatenate([np.zeros(1), np.cumsum(terms)]) + 0.5 * math.log(0.5)).astype(np.float32)
    colat = latitudes()
    weight = np.pi * np.sin(colat) * math.sqrt(NLAT) / (NLAT + 0.5)
    colat = np.stack([np.cos(colat), np.log(np.sin(colat)), weight]).astype(np.float32)
    rsel, csel = selections()
    table = (PAIRS, STEPS, 1280)
    block = vmem((PAIRS, CHUNK, 1280), lambda g, d: (0, g, 0))
    maps = (20, 128, 512)
    whole = lambda g, d: (0, 0, 0)
    own = pl.BlockSpec((None, 1, 10 * STEPS), lambda g, d: (d[0], 0, 0), memory_space=pltpu.SMEM)
    return pl.pallas_call(
        table_kernel,
        out_shape=tuple(jax.ShapeDtypeStruct(made, BF16) for made in (table, maps)),
        grid_spec=pltpu.PrefetchScalarGridSpec(
            num_scalar_prefetch=1,
            grid=(STEPS // CHUNK,),
            in_specs=[SMEM, SMEM, own] + [vmem()] * 5,
            out_specs=(block, vmem(maps, whole)),
            scratch_shapes=[
                pltpu.VMEM((2 * PAIRS, 8, 128), F32),
                pltpu.VMEM((2 * PAIRS, 8, 128), F32),
                pltpu.VMEM((PAIRS, 128, 128), F32),
            ],
        ),
        compiler_params=params(57),
        cost_estimate=cost(60_000_000, 60_000_000),
        name="legendre_table",
    )(
        device, codes, jnp.asarray(logs), jnp.asarray(recurrence_factors()), jnp.asarray(colat), row_map, col_map,
        jnp.asarray(rsel), jnp.asarray(csel),
    )


def body(source, row_map, col_map, pattern, codes, need_list, owner):
    lat_me = lax.axis_index("lat").astype(jnp.int32)
    tile_me = lax.axis_index("tile").astype(jnp.int32)
    device = tile_me * lax.axis_size("lat") + lat_me
    first = device * PAIRS
    me = lat_me.reshape(1)
    needs = need_list[0]
    outgoing = pl.pallas_call(
        pack_kernel,
        out_shape=jax.ShapeDtypeStruct((8 * MOST, 64, 512), BF16),
        in_specs=[SMEM, SMEM, SMEM, HBM],
        out_specs=HBM,
        scratch_shapes=[
            pltpu.VMEM((7, 8, 4096), BF16),
            pltpu.VMEM((2, 256, 128), F32),
            pltpu.VMEM((7, 64, 512), BF16),
            pltpu.SMEM((8 * MOST + 1,), jnp.int32),
            pltpu.SemaphoreType.DMA((7 + 8 * MOST,)),
        ],
        compiler_params=params(57),
        cost_estimate=cost(1_000_000, 2_000_000),
        name="pack",
    )(owner, needs, me, source)
    incoming = lax.all_to_all(outgoing, "lat", split_axis=0, concat_axis=0, tiled=True)

    code = jnp.transpose(codes, (1, 2, 0))
    table, maps = legendre_table(
        device.reshape(1), code, row_map.reshape(20, 32, 64), col_map.reshape(20, 64, 160)
    )

    field = pl.pallas_call(
        regrid_kernel,
        out_shape=jax.ShapeDtypeStruct((16, 112, 128), BF16),
        in_specs=[SMEM] * 5 + [vmem(), HBM],
        out_specs=vmem(),
        scratch_shapes=[
            pltpu.VMEM((20, 128, 512), BF16),
            pltpu.SemaphoreType.DMA((5,)),
            pltpu.VMEM((2 * NEED, 512, 128), BF16),
            pltpu.VMEM((2, 256, 128), F32),
            pltpu.VMEM((2, 256, 128), F32),
            pltpu.VMEM((16, 16, 128), F32),
            pltpu.SMEM((8,), jnp.int32),
        ],
        compiler_params=params(50),
        cost_estimate=cost(700_000_000, 5_000_000),
        name="regrid",
    )(owner, needs, me, jnp.transpose(pattern, (1, 2, 0)), code, incoming, maps)
    rows = lax.all_to_all(field, "tile", split_axis=0, concat_axis=0, tiled=True)

    spectral = pl.pallas_call(
        dft_kernel,
        out_shape=jax.ShapeDtypeStruct((128, 16, 128), BF16),
        in_specs=[vmem(), HBM],
        out_specs=vmem(),
        scratch_shapes=[
            pltpu.VMEM((5, 2, 2, 1280, 256), BF16),
            pltpu.SemaphoreType.DMA((5,)),
            pltpu.VMEM((2, 160, 1280), BF16),
            pltpu.VMEM((1664, 128), F32),
            pltpu.VMEM((2048, 128), F32),
        ],
        compiler_params=params(50),
        cost_estimate=cost(1_000_000_000, 14_000_000),
        name="dft",
    )(rows, jnp.asarray(dft_tables()))
    arranged = lax.all_to_all(spectral, ("lat", "tile"), split_axis=0, concat_axis=0, tiled=True)

    return pl.pallas_call(
        sums_kernel,
        out_shape=jax.ShapeDtypeStruct((PAIRS, 2 * LEV, M + 1), F32),
        in_specs=[SMEM, vmem(), HBM],
        out_specs=HBM,
        scratch_shapes=[
            pltpu.VMEM((PAIRS, STEPS, 1280), BF16),
            pltpu.VMEM((PAIRS, 2 * LEV, M + 1), F32),
            pltpu.SemaphoreType.DMA((2 * PAIRS,)),
            pltpu.VMEM((2048, 128), F32),
            pltpu.VMEM((1664, 128), F32),
            pltpu.VMEM((PAIRS, 64, 1280), BF16),
        ],
        compiler_params=params(50),
        cost_estimate=cost(2_000_000_000, 17_000_000),
        name="sums",
    )(first.reshape(1), arranged, table)


def solution(mesh):
    placed = (
        P(("tile", "lat"), None, None),
        P("lat", "tile", None, None, None),
        P("lat", None, None, "tile"),
        P("lat", "tile", None),
        P("lat", "tile", None),
        P("tile", None, None),
        P(),
    )
    return jax.shard_map(
        body, mesh=mesh, in_specs=placed, out_specs=P(("tile", "lat"), None, None), check_vma=False
    )
```

time: 96.2 us -> 91.7 us (0.953)
  Pallas kernels: 48.5 us -> 46.1 us
  local copies, waits for them, and re-layouts: 1.97 us -> 0.02 us
    unnamed x4 -> x8, local copies, waits for them, and re-layouts: 1.97 us -> 0.02 us
    pallas_call x2, Pallas kernels: 17 us -> 15.3 us  [the longest x1 8.88 us: body(): pl.pallas_call(sums_kernel, out_shape=jax.ShapeDtypeStruct((PAIRS, 2 * LE...]
  transfers between devices with their start and end apart: 2 -> 2, of which waited for: 2 -> 2; matrix products, arithmetic and copies ran while one was open for 0% -> 0% of each run, Pallas kernels for 19% -> 20%
where the time goes in v3:
time: 91.7 us; the launch traced here: 91.2 us
  Pallas kernels  46.1 us (50%)
  waiting for transfers between devices  16.2 us (18%)
  blocking collectives  15.2 us (17%)
  starting transfers between devices  13.5 us (15%)
    pallas_call x1, Pallas kernels, legendre_table(): pl.pallas_call(table_kernel, out_shape=tuple((jax.ShapeDtypeStruct(made,...  17.8 us
    all_to_all x1, blocking collectives, body(): lax.all_to_all(field, 'tile', split_axis=0, concat_axis=0, tiled=True)  15.2 us
    all_to_all x1, waiting for transfers between devices, body(): lax.all_to_all(spectral, ('lat', 'tile'), split_axis=0, concat_axis=0, ti...  13.3 us
    pallas_call x1, Pallas kernels, body(): pl.pallas_call(sums_kernel, out_shape=jax.ShapeDtypeStruct((PAIRS, 2 * LE...  8.88 us
    pallas_call x1, Pallas kernels, body(): pl.pallas_call(regrid_kernel, out_shape=jax.ShapeDtypeStruct((16, 112, 12...  8.66 us
    all_to_all x1, starting transfers between devices, body(): lax.all_to_all(outgoing, 'lat', split_axis=0, concat_axis=0, tiled=True)  6.83 us
    all_to_all x1, starting transfers between devices, body(): lax.all_to_all(spectral, ('lat', 'tile'), split_axis=0, concat_axis=0, ti...  6.69 us
    pallas_call x1, Pallas kernels, body(): pl.pallas_call(dft_kernel, out_shape=jax.ShapeDtypeStruct((128, 16, 128),...  6.43 us
  transfers between devices with their start and end apart: 2, of which 2 were waited for; matrix products, arithmetic and copies ran while one was open for 0% of the time, Pallas kernels for 20%

profile of v3, /device:TPU:1, one launch (start us, length us, event | category | flops | bytes accessed | tf_op | source)
XLA Modules:
  0.0 91.2 jit_solution(15987053245070352643)
XLA Ops:
  0.0 0.0 copy-start
  0.0 0.0 copy-start.1
  0.0 0.0 copy-start.2
  0.0 0.0 copy-start.3
  0.0 4.3 %pack.1 = bf16[24,64,512]{2,1,0:T(8,128)(2,1)} custom-call(s32[896]{0:T(1024)} %owner_ref.3, s32[8,12]{1,0:T(8,128)} %bitcast.8, s32[1]{0:T(128)} %bitcast.2.me_ref, bf16[7,8,4096]{2,1,0:T(8,128)(2,1)} %source_hbm.1), custom_call_target="tpu_custom_call" | custom-call | flops 1000000 | bytes 2000000 | tf_op jit(solution)/shard_map/pack/pallas_call | solution.py:422
  4.3 6.8 %all-to-all-start = ((bf16[24,64,512]{2,1,0:T(8,128)(2,1)}), bf16[24,64,512]{2,1,0:T(8,128)(2,1)S(1)}, u32[]{:S(2)}, u32[]{:S(2)}) async-start(bf16[24,64,512]{2,1,0:T(8,128)(2,1)} %pack.1), calls=%async_computation | async-start | bytes 3145728 | tf_op jit(solution)/shard_map/all_to_all | solution.py:438
  11.2 17.8 %legendre_table.1 = (bf16[5,1296,1280]{2,1,0:T(8,128)(2,1)}, bf16[20,128,512]{2,1,0:T(8,128)(2,1)}) custom-call(s32[1]{0:T(128)} %bitcast.5.device_ref, s32[1,4,5]{2,1,0:T(4,128)} %bitcast.10, f32[1280]{0:T(1024)} %constant.25.clone.logs_ref, f32[128,1,12960]{2,1,0:T(1,128)} %constant.26.clone.coef_ref, f32[3,8,128]{2,1,0:T(8,128)} %constant.27.clone.colat_ref, ...), custom_call_target="tpu_custom_call" | custom-call | flops 60000000 | bytes 60000000 | tf_op jit(solution)/shard_map/legendre_table/pallas_call | solution.py:392
  29.0 2.9 %all-to-all-done.blocks_ref = bf16[24,64,512]{2,1,0:T(8,128)(2,1)S(1)} async-done(((bf16[24,64,512]{2,1,0:T(8,128)(2,1)}), bf16[24,64,512]{2,1,0:T(8,128)(2,1)S(1)}, u32[]{:S(2)}, u32[]{:S(2)}) %all-to-all-start) | async-done | bytes 1572896 | tf_op jit(solution)/shard_map/all_to_all | solution.py:438
  31.9 0.0 copy-done
  31.9 0.0 copy-done.1
  31.9 0.0 copy-done.2
  31.9 0.0 copy-done.3
  31.9 8.7 %regrid.1 = bf16[16,112,128]{2,1,0:T(8,128)(2,1)S(1)} custom-call(s32[896]{0:T(1024)S(1)} %copy-done, s32[8,12]{1,0:T(8,128)S(1)} %bitcast.9, s32[1]{0:T(128)} %bitcast.2.me_ref, s32[1,4,5]{2,1,0:T(4,128)S(1)} %bitcast.12, s32[1,4,5]{2,1,0:T(4,128)S(1)} %bitcast.11, bf16[24,64,512]{2,1,0:T(8,128)(2,1)S(1)} %all-to-all-done.blocks_ref, ...), custom_call_target="tpu_custom_call" | custom-call | flops 700000000 | bytes 5000000 | tf_op jit(solution)/shard_map/regrid/pallas_call | solution.py:445
  40.6 15.2 %all_to_all.15.rows_ref = bf16[16,112,128]{2,1,0:T(8,128)(2,1)S(1)} all-to-all(bf16[16,112,128]{2,1,0:T(8,128)(2,1)S(1)} %regrid.1), channel_id=1, replica_groups=mesh['tile'=16,'lat'=8] {'tile'}, dimensions={0} | all-to-all | bytes 917504 | tf_op jit(solution)/shard_map/all_to_all | solution.py:463
  55.7 6.4 %dft.1 = bf16[128,16,128]{2,1,0:T(8,128)(2,1)} custom-call(bf16[16,112,128]{2,1,0:T(8,128)(2,1)S(1)} %all_to_all.15.rows_ref, bf16[5,2,2,1280,256]{4,3,2,1,0:T(8,128)(2,1)} %constant.30.clone.table_hbm), custom_call_target="tpu_custom_call" | custom-call | flops 1000000000 | bytes 14000000 | tf_op jit(solution)/shard_map/dft/pallas_call | solution.py:465
  62.2 6.7 %all-to-all-start.2 = ((bf16[128,16,128]{2,1,0:T(8,128)(2,1)}), bf16[128,16,128]{2,1,0:T(8,128)(2,1)S(1)}, u32[]{:S(2)}, u32[]{:S(2)}) async-start(bf16[128,16,128]{2,1,0:T(8,128)(2,1)} %dft.1), calls=%async_computation.2 | async-start | bytes 1048576 | tf_op jit(solution)/shard_map/all_to_all | solution.py:481
  68.9 13.3 %all-to-all-done.2.blocks_ref = bf16[128,16,128]{2,1,0:T(8,128)(2,1)S(1)} async-done(((bf16[128,16,128]{2,1,0:T(8,128)(2,1)}), bf16[128,16,128]{2,1,0:T(8,128)(2,1)S(1)}, u32[]{:S(2)}, u32[]{:S(2)}) %all-to-all-start.2) | async-done | bytes 524320 | tf_op jit(solution)/shard_map/all_to_all | solution.py:481
  82.2 8.9 %sums.1 = f32[5,16,1281]{2,1,0:T(8,128)} custom-call(s32[1]{0:T(128)} %bitcast.first_ref, bf16[128,16,128]{2,1,0:T(8,128)(2,1)S(1)} %all-to-all-done.2.blocks_ref, bf16[5,1296,1280]{2,1,0:T(8,128)(2,1)} %get-tuple-element.8.table_hbm), custom_call_target="tpu_custom_call" | custom-call | flops 2000000000 | bytes 17000000 | tf_op jit(solution)/shard_map/sums/pallas_call | solution.py:483
Async XLA Ops:
  0.0 31.9 %copy-start = (s32[896]{0:T(1024)S(1)}, s32[896]{0:T(1024)}, u32[]{:S(2)}) copy-start(s32[896]{0:T(1024)} %owner_ref.3) | copy-start | bytes 10756
  0.0 31.9 %copy-start.1 = (s32[1,8,12]{2,1,0:T(8,128)S(1)}, s32[1,8,12]{2,1,0:T(8,128)}, u32[]{:S(2)}) copy-start(s32[1,8,12]{2,1,0:T(8,128)} %param.18) | copy-start | bytes 1156
  0.0 31.9 %copy-start.2 = (s32[5,1,4]{0,2,1:T(4,128)S(1)}, s32[5,1,4]{0,2,1:T(4,128)}, u32[]{:S(2)}) copy-start(s32[5,1,4]{0,2,1:T(4,128)} %param.17) | copy-start | bytes 244
  0.0 31.9 %copy-start.3 = (s32[5,1,4]{0,2,1:T(4,128)S(1)}, s32[5,1,4]{0,2,1:T(4,128)}, u32[]{:S(2)}) copy-start(s32[5,1,4]{0,2,1:T(4,128)} %param.16) | copy-start | bytes 244
  4.3 27.5 %all-to-all-start = ((bf16[24,64,512]{2,1,0:T(8,128)(2,1)}), bf16[24,64,512]{2,1,0:T(8,128)(2,1)S(1)}, u32[]{:S(2)}, u32[]{:S(2)}) async-start(bf16[24,64,512]{2,1,0:T(8,128)(2,1)} %pack.1), calls=%async_computation | async-start | bytes 3145728 | tf_op jit(solution)/shard_map/all_to_all | solution.py:438
  62.2 20.0 %all-to-all-start.2 = ((bf16[128,16,128]{2,1,0:T(8,128)(2,1)}), bf16[128,16,128]{2,1,0:T(8,128)(2,1)S(1)}, u32[]{:S(2)}, u32[]{:S(2)}) async-start(bf16[128,16,128]{2,1,0:T(8,128)(2,1)} %dft.1), calls=%async_computation.2 | async-start | bytes 1048576 | tf_op jit(solution)/shard_map/all_to_all | solution.py:481

commit v4 on v3

--- a/solution.py
+++ b/solution.py
@@ -100,23 +100,18 @@
 
 
 def regrid_kernel(
-    owner_ref, need_ref, me_ref, pattern_ref, codes_ref, blocks_ref, maps_hbm, out_ref,
-    maps_ref, sems, forms_ref, acc_ref, tail_ref, packed_ref, seen_ref,
+    owner_ref, need_ref, me_ref, pattern_ref, codes_ref, blocks_ref, cols_ref, wide_ref, out_ref,
+    forms_ref, acc_ref, tail_ref, packed_ref, seen_ref,
 ):
     me = me_ref[0]
     south = me >= 4
     row_blocks = [jnp.where(south, 4 - b, b) for b in range(5)]
-    loads = [
-        pltpu.make_async_copy(maps_hbm.at[pl.ds(row_blocks[b] * 4, 4)], maps_ref.at[b * 4 : b * 4 + 4], sems.at[b])
-        for b in range(5)
-    ]
-    for load in loads:
-        load.start()
     for l in range(8):
         seen_ref[l] = 0
     tail_ref[...] = jnp.zeros_like(tail_ref)
     lane = lax.broadcasted_iota(jnp.int32, (64, 128), 1)
     zero = jnp.zeros((64, 128), BF16)
+    diagonal = lax.broadcasted_iota(jnp.int32, (128, 256), 0) // 32 == lax.broadcasted_iota(jnp.int32, (128, 256), 1) // 64
     places = []
     for i in range(NEED):
         lat, _ = holder_of(owner_ref, need_ref, me, i)
@@ -138,16 +133,14 @@
                     forms_ref[2 * i + 1, at + half * 64 : at + half * 64 + 64, :] = picked
 
     for b in range(5):
-        loads[b].wait()
         sums = [None, None]
         for k in range(4):
-            term = b * 4 + k
+            term = row_blocks[b] * 4 + k
             form = forms_ref[pattern_ref[0, k, row_blocks[b]] * 2 + (codes_ref[0, k, row_blocks[b]] & 1)]
-            inner = jnp.dot(form, maps_ref[term, :, 0:160], preferred_element_type=F32).astype(BF16)
+            rows = jnp.where(diagonal, jnp.concatenate([wide_ref[term]] * 4, axis=0), jnp.zeros((128, 256), BF16))
+            inner = jnp.dot(form, cols_ref[term], preferred_element_type=F32).astype(BF16)
             for half in range(2):
-                new = jnp.dot(
-                    maps_ref[term, :, 256:512], inner[half * 256 : (half + 1) * 256], preferred_element_type=F32
-                )
+                new = jnp.dot(rows, inner[half * 256 : (half + 1) * 256], preferred_element_type=F32)
                 sums[half] = new if k == 0 else sums[half] + new
         for half in range(2):
             acc_ref[b % 2, half * 128 : (half + 1) * 128, :] = sums[half][:, :128]
@@ -223,8 +216,8 @@
 
 
 def table_kernel(
-    device_ref, codes_ref, logs_ref, coef_ref, colat_ref, rmap_ref, cmap_ref, rsel_ref, csel_ref,
-    legendre_out, maps_out, state_ref, start_ref, rows_ref,
+    device_ref, codes_ref, coef_ref, colat_ref, rmap_ref, cmap_ref, select_ref,
+    legendre_out, cols_out, wide_out, state_ref, start_ref, rows_ref,
 ):
     step = pl.program_id(0)
     first = device_ref[0] * PAIRS
@@ -236,17 +229,13 @@
         for i in range(PAIRS):
             for h in range(2):
                 order = first + i if h == 0 else M - 1 - first - i
-                exponent = logs_ref[order] + order.astype(F32) * log_sine
+                exponent = coef_ref[0, 10 * STEPS + h * PAIRS + i] + order.astype(F32) * log_sine
                 ramp = jnp.clip((exponent + 75.0) / 10.0, 0.0, 1.0)
                 start_ref[h * PAIRS + i] = jnp.exp(jnp.maximum(exponent, -75.0)) * ramp * weight
-        sub = lax.broadcasted_iota(jnp.int32, (128, 256), 0) // 32
-        lane = lax.broadcasted_iota(jnp.int32, (128, 256), 1) // 64
         for term in range(20):
             code = codes_ref[0, term % 4, term // 4]
-            wide = jnp.dot(rmap_ref[term], rsel_ref[code], preferred_element_type=F32)
-            wide = jnp.concatenate([wide] * 4, axis=0)
-            maps_out[term, :, 256:512] = jnp.where(sub == lane, wide, 0.0).astype(BF16)
-            maps_out[term, :, 0:160] = jnp.dot(csel_ref[code], cmap_ref[term], preferred_element_type=F32).astype(BF16)
+            wide_out[term] = jnp.dot(rmap_ref[term], select_ref[code, 0:64, :], preferred_element_type=F32).astype(BF16)
+            cols_out[term] = jnp.dot(select_ref[code, 64:192, 0:64], cmap_ref[term], preferred_element_type=F32).astype(BF16)
 
     cosine = colat_ref[0]
 
@@ -359,7 +348,11 @@
     n2, l2, m2 = degree.astype(np.float64) ** 2, (degree - 1.0) ** 2, order.astype(np.float64) ** 2
     grow = np.where(grows, np.sqrt(np.where(grows, 4 * n2 - 1, 0) / np.where(grows, n2 - m2, 1)), 0)
     keep = np.where(back, grow * np.sqrt(np.where(back, l2 - m2, 0) / np.where(back, 4 * l2 - 1, 1)), 0)
-    return np.stack([grow, keep], axis=1).astype(np.float32).reshape(128, 1, 10 * STEPS)
+    factors = np.stack([grow, keep], axis=1).reshape(128, 10 * STEPS)
+    terms = 0.5 * np.log1p(0.5 / np.arange(1, M, dtype=np.float64))
+    logs = np.concatenate([np.zeros(1), np.cumsum(terms)]) + 0.5 * math.log(0.5)
+    pair = pair.reshape(128, PAIRS)
+    return np.concatenate([factors, logs[pair], logs[M - 1 - pair]], axis=1).astype(np.float32)[:, None]
 
 
 def selections():
@@ -374,41 +367,38 @@
         cols = 63 - cols if code in (2, 3) else cols
         csel[code, np.arange(64), cols] = 1
         csel[code, 64 + np.arange(64), cols] = 1
-    return rsel.astype(BF16), csel.astype(BF16)
+    csel = np.concatenate([csel, np.zeros((4, 128, 192))], axis=2)
+    return np.concatenate([rsel, csel], axis=1).astype(BF16)
 
 
 def legendre_table(device, codes, row_map, col_map):
-    terms = 0.5 * np.log1p(0.5 / np.arange(1, M, dtype=np.float64))
-    logs = (np.concatenate([np.zeros(1), np.cumsum(terms)]) + 0.5 * math.log(0.5)).astype(np.float32)
     colat = latitudes()
     weight = np.pi * np.sin(colat) * math.sqrt(NLAT) / (NLAT + 0.5)
     colat = np.stack([np.cos(colat), np.log(np.sin(colat)), weight]).astype(np.float32)
-    rsel, csel = selections()
     table = (PAIRS, STEPS, 1280)
     block = vmem((PAIRS, CHUNK, 1280), lambda g, d: (0, g, 0))
-    maps = (20, 128, 512)
+    cols, wide = (20, 128, 160), (20, 32, 256)
     whole = lambda g, d: (0, 0, 0)
-    own = pl.BlockSpec((None, 1, 10 * STEPS), lambda g, d: (d[0], 0, 0), memory_space=pltpu.SMEM)
+    own = pl.BlockSpec((None, 1, 10 * STEPS + 2 * PAIRS), lambda g, d: (d[0], 0, 0), memory_space=pltpu.SMEM)
     return pl.pallas_call(
         table_kernel,
-        out_shape=tuple(jax.ShapeDtypeStruct(made, BF16) for made in (table, maps)),
+        out_shape=tuple(jax.ShapeDtypeStruct(made, BF16) for made in (table, cols, wide)),
         grid_spec=pltpu.PrefetchScalarGridSpec(
             num_scalar_prefetch=1,
             grid=(STEPS // CHUNK,),
-            in_specs=[SMEM, SMEM, own] + [vmem()] * 5,
-            out_specs=(block, vmem(maps, whole)),
+            in_specs=[SMEM, own] + [vmem()] * 4,
+            out_specs=(block, vmem(cols, whole), vmem(wide, whole)),
             scratch_shapes=[
                 pltpu.VMEM((2 * PAIRS, 8, 128), F32),
                 pltpu.VMEM((2 * PAIRS, 8, 128), F32),
                 pltpu.VMEM((PAIRS, 128, 128), F32),
             ],
         ),
-        compiler_params=params(57),
+        compiler_params=params(50),
         cost_estimate=cost(60_000_000, 60_000_000),
         name="legendre_table",
     )(
-        device, codes, jnp.asarray(logs), jnp.asarray(recurrence_factors()), jnp.asarray(colat), row_map, col_map,
-        jnp.asarray(rsel), jnp.asarray(csel),
+        device, codes, jnp.asarray(recurrence_factors()), jnp.asarray(colat), row_map, col_map, jnp.asarray(selections()),
     )
 
 
@@ -438,28 +428,26 @@
     incoming = lax.all_to_all(outgoing, "lat", split_axis=0, concat_axis=0, tiled=True)
 
     code = jnp.transpose(codes, (1, 2, 0))
-    table, maps = legendre_table(
+    table, cols, wide = legendre_table(
         device.reshape(1), code, row_map.reshape(20, 32, 64), col_map.reshape(20, 64, 160)
     )
 
     field = pl.pallas_call(
         regrid_kernel,
         out_shape=jax.ShapeDtypeStruct((16, 112, 128), BF16),
-        in_specs=[SMEM] * 5 + [vmem(), HBM],
+        in_specs=[SMEM] * 5 + [vmem()] * 3,
         out_specs=vmem(),
         scratch_shapes=[
-            pltpu.VMEM((20, 128, 512), BF16),
-            pltpu.SemaphoreType.DMA((5,)),
             pltpu.VMEM((2 * NEED, 512, 128), BF16),
             pltpu.VMEM((2, 256, 128), F32),
             pltpu.VMEM((2, 256, 128), F32),
             pltpu.VMEM((16, 16, 128), F32),
             pltpu.SMEM((8,), jnp.int32),
         ],
-        compiler_params=params(50),
+        compiler_params=params(14),
         cost_estimate=cost(700_000_000, 5_000_000),
         name="regrid",
-    )(owner, needs, me, jnp.transpose(pattern, (1, 2, 0)), code, incoming, maps)
+    )(owner, needs, me, jnp.transpose(pattern, (1, 2, 0)), code, incoming, cols, wide)
     rows = lax.all_to_all(field, "tile", split_axis=0, concat_axis=0, tiled=True)
 
     spectral = pl.pallas_call(

time: 91.7 us -> 92.2 us (level)
  local copies, waits for them, and re-layouts: 0.02 us -> 4.4 us
  Pallas kernels: 46.1 us -> 43 us
  waiting for transfers between devices: 16.2 us -> 13.3 us
  blocking collectives: 15.2 us -> 16.3 us
    unnamed x8 -> x18, local copies, waits for them, and re-layouts: 0.02 us -> 4.4 us
    all_to_all x1, waiting for transfers between devices: 2.89 us -> 0.01 us  [body(): lax.all_to_all(outgoing, 'lat', split_axis=0, concat_axis=0, tiled=True)]
    pallas_call x1, Pallas kernels: 8.66 us -> 6.74 us  [body(): pl.pallas_call(regrid_kernel, out_shape=jax.ShapeDtypeStruct((16, 112, 12...]
    pallas_call x1, Pallas kernels: 17.8 us -> 16.6 us  [legendre_table(): pl.pallas_call(table_kernel, out_shape=tuple((jax.ShapeDtypeStruct(made,...]
    all_to_all x1, blocking collectives: 15.2 us -> 16.3 us  [body(): lax.all_to_all(field, 'tile', split_axis=0, concat_axis=0, tiled=True)]
  transfers between devices with their start and end apart: 2 -> 2, of which waited for: 2 -> 1; matrix products, arithmetic and copies ran while one was open for 0% -> 0% of each run, Pallas kernels for 20% -> 18%
where the time goes in v4:
time: 92.2 us; the launch traced here: 91.6 us
  Pallas kernels  43 us (47%)
  blocking collectives  16.3 us (18%)
  starting transfers between devices  14.4 us (16%)
  waiting for transfers between devices  13.3 us (14%)
  local copies, waits for them, and re-layouts  4.4 us (5%)
    pallas_call x1, Pallas kernels, legendre_table(): pl.pallas_call(table_kernel, out_shape=tuple((jax.ShapeDtypeStruct(made,...  16.6 us
    all_to_all x1, blocking collectives, body(): lax.all_to_all(field, 'tile', split_axis=0, concat_axis=0, tiled=True)  16.3 us
    all_to_all x1, waiting for transfers between devices, body(): lax.all_to_all(spectral, ('lat', 'tile'), split_axis=0, concat_axis=0, ti...  13.3 us
    pallas_call x1, Pallas kernels, body(): pl.pallas_call(sums_kernel, out_shape=jax.ShapeDtypeStruct((PAIRS, 2 * LE...  8.87 us
    all_to_all x1, starting transfers between devices, body(): lax.all_to_all(spectral, ('lat', 'tile'), split_axis=0, concat_axis=0, ti...  7.55 us
    all_to_all x1, starting transfers between devices, body(): lax.all_to_all(outgoing, 'lat', split_axis=0, concat_axis=0, tiled=True)  6.83 us
    pallas_call x1, Pallas kernels, body(): pl.pallas_call(regrid_kernel, out_shape=jax.ShapeDtypeStruct((16, 112, 12...  6.74 us
    pallas_call x1, Pallas kernels, body(): pl.pallas_call(dft_kernel, out_shape=jax.ShapeDtypeStruct((128, 16, 128),...  6.44 us
  transfers between devices with their start and end apart: 2, of which 1 were waited for; matrix products, arithmetic and copies ran while one was open for 0% of the time, Pallas kernels for 18%

profile of v4, /device:TPU:1, one launch (start us, length us, event | category | flops | bytes accessed | tf_op | source)
XLA Modules:
  0.0 91.6 jit_solution(161180950665081632)
XLA Ops:
  0.0 0.0 copy-start.3
  0.0 0.0 copy-start.4
  0.0 0.0 copy-start.7
  0.0 0.0 copy-start.8
  0.0 4.3 %pack.1 = bf16[24,64,512]{2,1,0:T(8,128)(2,1)} custom-call(s32[896]{0:T(1024)} %owner_ref.3, s32[8,12]{1,0:T(8,128)} %bitcast.10, s32[1]{0:T(128)} %bitcast.2.me_ref, bf16[7,8,4096]{2,1,0:T(8,128)(2,1)} %source_hbm.1), custom_call_target="tpu_custom_call" | custom-call | flops 1000000 | bytes 2000000 | tf_op jit(solution)/shard_map/pack/pallas_call | solution.py:412
  4.4 6.8 %all-to-all-start = ((bf16[24,64,512]{2,1,0:T(8,128)(2,1)}), bf16[24,64,512]{2,1,0:T(8,128)(2,1)S(1)}, u32[]{:S(2)}, u32[]{:S(2)}) async-start(bf16[24,64,512]{2,1,0:T(8,128)(2,1)} %pack.1), calls=%async_computation | async-start | bytes 3145728 | tf_op jit(solution)/shard_map/all_to_all | solution.py:428
  11.2 0.0 copy-start
  11.2 1.1 %copy-done = bf16[5,4,64,160]{3,2,1,0:T(8,128)(2,1)S(1)} copy-done((bf16[5,4,64,160]{3,2,1,0:T(8,128)(2,1)S(1)}, bf16[5,4,64,160]{3,2,1,0:T(8,128)(2,1)}, u32[]{:S(2)}) %copy-start) | copy-done | bytes 409624
  12.3 0.0 copy-start.1
  12.3 1.0 %copy-done.1 = bf16[4,192,256]{2,1,0:T(8,128)(2,1)S(1)} copy-done((bf16[4,192,256]{2,1,0:T(8,128)(2,1)S(1)}, bf16[4,192,256]{2,1,0:T(8,128)(2,1)}, u32[]{:S(2)}) %copy-start.1) | copy-done | bytes 393240
  13.3 0.0 copy-start.2
  13.3 0.9 copy-done.2
  14.2 0.0 copy-start.5
  14.2 0.7 copy-done.5
  14.9 0.0 copy-start.6
  14.9 0.7 copy-done.6
  15.6 16.6 %legendre_table.1 = (bf16[5,1296,1280]{2,1,0:T(8,128)(2,1)}, bf16[20,128,160]{2,1,0:T(8,128)(2,1)S(1)}, bf16[20,32,256]{2,1,0:T(8,128)(2,1)S(1)}) custom-call(s32[1]{0:T(128)} %bitcast.5.device_ref, s32[1,4,5]{2,1,0:T(4,128)S(1)} %bitcast.12, f32[128,1,12970]{2,1,0:T(1,128)} %constant.21.clone.coef_ref, f32[3,8,128]{2,1,0:T(8,128)S(1)} %copy-done.5, ...), custom_call_target="tpu_custom_call" | custom-call | flops 60000000 | bytes 60000000 | tf_op jit(solution)/shard_map/legendre_table/pallas_call | solution.py:383
  32.2 0.0 all-to-all-done.blocks_ref
  32.2 0.0 copy-done.3
  32.2 0.0 copy-done.4
  32.2 0.0 copy-done.7
  32.2 0.0 copy-done.8
  32.2 6.7 %regrid.1 = bf16[16,112,128]{2,1,0:T(8,128)(2,1)S(1)} custom-call(s32[896]{0:T(1024)S(1)} %copy-done.3, s32[8,12]{1,0:T(8,128)S(1)} %bitcast.11, s32[1]{0:T(128)} %bitcast.2.me_ref, s32[1,4,5]{2,1,0:T(4,128)S(1)} %bitcast.14, s32[1,4,5]{2,1,0:T(4,128)S(1)} %bitcast.13, bf16[24,64,512]{2,1,0:T(8,128)(2,1)S(1)} %all-to-all-done.blocks_ref, ...), custom_call_target="tpu_custom_call" | custom-call | flops 700000000 | bytes 5000000 | tf_op jit(solution)/shard_map/regrid/pallas_call | solution.py:435
  39.0 16.3 %all_to_all.15.rows_ref = bf16[16,112,128]{2,1,0:T(8,128)(2,1)S(1)} all-to-all(bf16[16,112,128]{2,1,0:T(8,128)(2,1)S(1)} %regrid.1), channel_id=1, replica_groups=mesh['tile'=16,'lat'=8] {'tile'}, dimensions={0} | all-to-all | bytes 917504 | tf_op jit(solution)/shard_map/all_to_all | solution.py:451
  55.3 6.4 %dft.1 = bf16[128,16,128]{2,1,0:T(8,128)(2,1)} custom-call(bf16[16,112,128]{2,1,0:T(8,128)(2,1)S(1)} %all_to_all.15.rows_ref, bf16[5,2,2,1280,256]{4,3,2,1,0:T(8,128)(2,1)} %constant.24.clone.table_hbm), custom_call_target="tpu_custom_call" | custom-call | flops 1000000000 | bytes 14000000 | tf_op jit(solution)/shard_map/dft/pallas_call | solution.py:453
  61.7 7.6 %all-to-all-start.2 = ((bf16[128,16,128]{2,1,0:T(8,128)(2,1)}), bf16[128,16,128]{2,1,0:T(8,128)(2,1)S(1)}, u32[]{:S(2)}, u32[]{:S(2)}) async-start(bf16[128,16,128]{2,1,0:T(8,128)(2,1)} %dft.1), calls=%async_computation.2 | async-start | bytes 1048576 | tf_op jit(solution)/shard_map/all_to_all | solution.py:469
  69.3 13.3 %all-to-all-done.2.blocks_ref = bf16[128,16,128]{2,1,0:T(8,128)(2,1)S(1)} async-done(((bf16[128,16,128]{2,1,0:T(8,128)(2,1)}), bf16[128,16,128]{2,1,0:T(8,128)(2,1)S(1)}, u32[]{:S(2)}, u32[]{:S(2)}) %all-to-all-start.2) | async-done | bytes 524320 | tf_op jit(solution)/shard_map/all_to_all | solution.py:469
  82.6 8.9 %sums.1 = f32[5,16,1281]{2,1,0:T(8,128)} custom-call(s32[1]{0:T(128)} %bitcast.first_ref, bf16[128,16,128]{2,1,0:T(8,128)(2,1)S(1)} %all-to-all-done.2.blocks_ref, bf16[5,1296,1280]{2,1,0:T(8,128)(2,1)} %get-tuple-element.10.table_hbm), custom_call_target="tpu_custom_call" | custom-call | flops 2000000000 | bytes 17000000 | tf_op jit(solution)/shard_map/sums/pallas_call | solution.py:471
Async XLA Ops:
  0.0 32.2 %copy-start.3 = (s32[896]{0:T(1024)S(1)}, s32[896]{0:T(1024)}, u32[]{:S(2)}) copy-start(s32[896]{0:T(1024)} %owner_ref.3) | copy-start | bytes 10756
  0.0 32.2 %copy-start.4 = (s32[1,8,12]{2,1,0:T(8,128)S(1)}, s32[1,8,12]{2,1,0:T(8,128)}, u32[]{:S(2)}) copy-start(s32[1,8,12]{2,1,0:T(8,128)} %param.16) | copy-start | bytes 1156
  0.0 32.2 %copy-start.7 = (s32[5,1,4]{0,2,1:T(4,128)S(1)}, s32[5,1,4]{0,2,1:T(4,128)}, u32[]{:S(2)}) copy-start(s32[5,1,4]{0,2,1:T(4,128)} %param.15) | copy-start | bytes 244
  0.0 32.2 %copy-start.8 = (s32[5,1,4]{0,2,1:T(4,128)S(1)}, s32[5,1,4]{0,2,1:T(4,128)}, u32[]{:S(2)}) copy-start(s32[5,1,4]{0,2,1:T(4,128)} %param.14) | copy-start | bytes 244
  4.4 27.8 %all-to-all-start = ((bf16[24,64,512]{2,1,0:T(8,128)(2,1)}), bf16[24,64,512]{2,1,0:T(8,128)(2,1)S(1)}, u32[]{:S(2)}, u32[]{:S(2)}) async-start(bf16[24,64,512]{2,1,0:T(8,128)(2,1)} %pack.1), calls=%async_computation | async-start | bytes 3145728 | tf_op jit(solution)/shard_map/all_to_all | solution.py:428
  11.2 1.1 %copy-start = (bf16[5,4,64,160]{3,2,1,0:T(8,128)(2,1)S(1)}, bf16[5,4,64,160]{3,2,1,0:T(8,128)(2,1)}, u32[]{:S(2)}) copy-start(bf16[5,4,64,160]{3,2,1,0:T(8,128)(2,1)} %param.13) | copy-start | bytes 1228804
  12.3 1.0 %copy-start.1 = (bf16[4,192,256]{2,1,0:T(8,128)(2,1)S(1)}, bf16[4,192,256]{2,1,0:T(8,128)(2,1)}, u32[]{:S(2)}) copy-start(bf16[4,192,256]{2,1,0:T(8,128)(2,1)} %constant.23.clone.select_ref) | copy-start | bytes 1179652
  13.3 0.9 copy-start.2
  14.2 0.7 copy-start.5
  14.9 0.7 copy-start.6
  61.7 20.9 %all-to-all-start.2 = ((bf16[128,16,128]{2,1,0:T(8,128)(2,1)}), bf16[128,16,128]{2,1,0:T(8,128)(2,1)S(1)}, u32[]{:S(2)}, u32[]{:S(2)}) async-start(bf16[128,16,128]{2,1,0:T(8,128)(2,1)} %dft.1), calls=%async_computation.2 | async-start | bytes 1048576 | tf_op jit(solution)/shard_map/all_to_all | solution.py:469
